TPU v7x, 32 devices: a whole 2x2x4 slice. The times are simulated.
32 devices in a mesh: row: 4 (over y, core), col: 8 (over z, x).
Axes of the slice: x: 2, y: 2, z: 4, core: 2. Of those that a mesh axis runs over, the one named last changes fastest.
Arguments:
- descriptors: bfloat16 [2048, 1024], P(('row', 'col'))
- gradients: bfloat16 [3, 4, 2048, 1024], P(None, None, ('row', 'col'))
- sparse_panel: bfloat16 [512, 1024], P('col')
- sparse_trail: bfloat16 [1024, 1024], P('col')
- atom_counts: int32 [32, 4], P(('row', 'col')), may hold values from 1 to 16, 32 in all within a row
- owner_rows: int32 [32, 4], P(('row', 'col')), may hold values from 0 to 3, each once within a row
- neighbor_ids: int32 [128, 16, 4], P(('row', 'col')), may hold values from 0 to 65519
Outputs:
- panel_factor: float32 [512, 512], replicated
- cross_factor: float32 [1024, 512], P('col')
- trail_residual: float32 [1024, 8192], P('col', 'row')
Inputs may be any that keep to these rules, and one draw needn't show every extreme that they name: `atom_counts`: the structures of one device's line hold 32 atoms together, and every line has a structure of 16 atoms. `owner_rows`: every device gives exactly one structure to each row group.
All inputs are finite; a program needn't handle non-finite values.
Results may differ from a plain program's by a relative error of at most 0.0043.
Values may be sent and summed in bfloat16 or wider, within the bound.
A program may use at most 128 MiB of HBM per device.

v0:
```python
import jax
import jax.numpy as jnp
from jax import lax
from jax.sharding import PartitionSpec as P

ridge_value = 0.1


def slot_rows(environments, desc_here, slope_here, count_here, neighbor_here, owner_here):
    struct_count = count_here.shape[0]
    atom_slots = neighbor_here.shape[1]
    neighbor_count = neighbor_here.shape[2]
    env_count = environments.shape[0]
    correlation = lax.dot_general(
        environments, desc_here, (((1,), (1,)), ((), ())), preferred_element_type=jnp.float32
    )
    slope_dots = lax.dot_general(
        environments, slope_here, (((1,), (1,)), ((), ())), preferred_element_type=jnp.float32
    )
    slope_dots = slope_dots.reshape(env_count, 3, neighbor_count, struct_count, atom_slots)
    slot_index = jnp.arange(atom_slots, dtype=jnp.int32)
    live_mask = (slot_index[None, :] < count_here[:, None]).astype(jnp.float32)
    squares = (correlation * correlation).reshape(env_count, struct_count, atom_slots)
    energy = jnp.sum(squares * live_mask[None], axis=2) / count_here.astype(jnp.float32)[None, :]
    partner = neighbor_here % count_here[:, None, None]
    struct_index = jnp.arange(struct_count, dtype=jnp.int32)
    flat_index = (struct_index[:, None, None] * atom_slots + partner).reshape(-1)
    picked = jnp.take(correlation, flat_index, axis=1).reshape(
        env_count, struct_count, atom_slots, neighbor_count
    )
    picked = jnp.transpose(picked, (0, 3, 1, 2))
    forces = -2.0 * jnp.sum(picked[:, None] * slope_dots, axis=2) * live_mask[None, None]
    forces = jnp.transpose(forces, (0, 2, 3, 1)).reshape(env_count, struct_count, 3 * atom_slots)
    padding = jnp.zeros((env_count, struct_count, atom_slots - 1), jnp.float32)
    slot_values = jnp.concatenate([energy[:, :, None], forces, padding], axis=2).astype(
        jnp.bfloat16
    )
    chosen = (owner_here[None, :] == struct_index[:, None]).astype(jnp.int32)
    owner_order = jnp.sum(struct_index[None, :] * chosen, axis=1)
    return jnp.take(slot_values, owner_order, axis=1)


def factor_panel(gram_sum, cross_sum, total_rows):
    gram_matrix = gram_sum / total_rows + ridge_value * jnp.eye(
        gram_sum.shape[0], dtype=jnp.float32
    )
    lower_factor = jnp.linalg.cholesky(gram_matrix)
    coupling = lax.linalg.triangular_solve(
        lower_factor, cross_sum / total_rows, left_side=True, lower=True
    )
    weights = lax.linalg.triangular_solve(
        lower_factor, coupling, left_side=True, lower=True, transpose_a=True
    )
    return (lower_factor.T, coupling, weights)


def split_weights(weights):
    weight_high = weights.astype(jnp.bfloat16)
    held_high = lax.optimization_barrier(weight_high)
    weight_low = (weights - held_high.astype(jnp.float32)).astype(jnp.bfloat16)
    return (weight_high, weight_low)


def reduce_products(gram_part, cross_part):
    return lax.psum((gram_part, cross_part), ("row", "col"))


def contract_rows(left_side, right_side):
    return lax.dot_general(
        left_side, right_side, (((1,), (1,)), ((), ())), preferred_element_type=jnp.float32
    )


def contract_cols(left_side, right_side):
    return lax.dot_general(
        left_side, right_side, (((0,), (0,)), ((), ())), preferred_element_type=jnp.float32
    )


def arrange_direct(block_rows, row_count, col_count):
    env_width = block_rows.shape[0] // col_count
    slot_count = block_rows.shape[2]
    shaped = block_rows.reshape(col_count, env_width, row_count, slot_count)
    return jnp.transpose(shaped, (2, 0, 1, 3)).reshape(row_count * col_count, env_width, slot_count)


def restore_direct(block_rows, row_count, col_count):
    env_width = block_rows.shape[1]
    slot_count = block_rows.shape[2]
    shaped = block_rows.reshape(row_count, col_count, env_width, slot_count)
    return jnp.transpose(shaped, (2, 1, 0, 3)).reshape(
        env_width, row_count * col_count * slot_count
    )


def per_device(
    descriptors, gradients, sparse_panel, sparse_trail, atom_counts, owner_rows, neighbor_ids
):
    row_count = lax.axis_size("row")
    col_count = lax.axis_size("col")
    col_index = lax.axis_index("col")
    count_here = atom_counts[0]
    owner_here = owner_rows[0]
    slope_here = gradients.reshape(-1, gradients.shape[3])
    panel_width = sparse_panel.shape[0]
    trail_width = sparse_trail.shape[0]
    panel_total = panel_width * col_count
    trail_total = trail_width * col_count
    slot_count = 4 * neighbor_ids.shape[1]
    total_rows = row_count * row_count * col_count * slot_count
    own_envs = jnp.concatenate([sparse_panel, sparse_trail], axis=0)
    kernel_rows = slot_rows(
        lax.all_gather(own_envs, "col", axis=0, tiled=True),
        descriptors,
        slope_here,
        count_here,
        neighbor_ids,
        owner_here,
    )
    blocks = kernel_rows.reshape(col_count, panel_width + trail_width, row_count, slot_count)
    panel_rows = blocks[:, :panel_width].reshape(panel_total, row_count, slot_count)
    trail_rows = blocks[:, panel_width:].reshape(trail_total, row_count, slot_count)
    received = (
        lax.all_to_all(
            arrange_direct(panel_rows, row_count, col_count),
            ("row", "col"),
            split_axis=0,
            concat_axis=0,
            tiled=True,
        ),
        lax.all_to_all(
            arrange_direct(trail_rows, row_count, col_count),
            ("row", "col"),
            split_axis=0,
            concat_axis=0,
            tiled=True,
        ),
    )
    panel_own = restore_direct(received[0], row_count, col_count)
    trail_own = restore_direct(received[1], row_count, col_count)
    segment = lax.all_gather(panel_own, "col", axis=0, tiled=True)
    columns = jnp.concatenate(
        [contract_rows(segment, panel_own), contract_rows(segment, trail_own)], axis=1
    )
    gram_part = lax.dynamic_update_slice(
        jnp.zeros((panel_total, panel_total), jnp.float32),
        columns[:, :panel_width],
        (0, col_index * panel_width),
    )
    cross_part = lax.dynamic_update_slice(
        jnp.zeros((panel_total, trail_total), jnp.float32),
        columns[:, panel_width:],
        (0, col_index * trail_width),
    )
    gram_sum, cross_sum = reduce_products(gram_part, cross_part)
    panel_factor, coupling, weights = factor_panel(gram_sum, cross_sum, total_rows)
    coupling_own = lax.dynamic_slice_in_dim(coupling, col_index * trail_width, trail_width, 1)
    weights_own = lax.dynamic_slice_in_dim(weights, col_index * trail_width, trail_width, 1)
    weight_high, weight_low = split_weights(weights_own)
    segment = lax.all_gather(panel_own, "col", axis=0, tiled=True)
    trail_residual = (
        trail_own.astype(jnp.float32)
        - contract_cols(weight_high, segment)
        - contract_cols(weight_low, segment)
    )
    cross_factor = coupling_own.T
    return (panel_factor, cross_factor, trail_residual)


def solution(mesh):
    return jax.shard_map(
        per_device,
        mesh=mesh,
        in_specs=(
            P(("row", "col"), None),
            P(None, None, ("row", "col"), None),
            P("col", None),
            P("col", None),
            P(("row", "col"), None),
            P(("row", "col"), None),
            P(("row", "col"), None, None),
        ),
        out_specs=(P(), P("col", None), P("col", "row")),
        check_vma=False,
    )
```

profile of v0, /device:TPU:0, one launch (start us, length us, event | category | flops | bytes accessed | tf_op | source)
XLA Modules:
  0.0 496.3 jit_solution(8556945889482428903)
XLA Ops:
  16.3 57.7 %all-gather.3.cloned.1.call-done = bf16[1536,1024]{1,0:T(8,128)(2,1)} async-done(((bf16[192,1024]{1,0:T(8,128)(2,1)}), bf16[1536,1024]{1,0:T(8,128)(2,1)}) %all-gather.3.cloned.1.call-update) | async-done | bytes 3145744 | tf_op jit(solution)/shard_map/all_gather | solution.py:113
  74.0 3.6 multiply_reduce_fusion.1
  80.4 2.1 fusion.13
  82.8 2.9 multiply_reduce_fusion
  92.9 13.8 %all_to_all.10 = bf16[32,2,2048]{2,1,0:T(2,128)(2,1)} all-to-all(bf16[32,2,2048]{2,1,0:T(2,128)(2,1)S(1)} %reshape.290), channel_id=1, replica_groups=mesh['row'=4,'col'=8] {'row','col'}, dimensions={0} | all-to-all | bytes 524288 | tf_op jit(solution)/shard_map/all_to_all | solution.py:124
  106.7 2.1 reshape.291
  108.8 2.2 copy.92
  111.0 2.2 reshape.250
  114.3 2.4 copy.79
  116.7 2.6 all-to-all-start.1
  119.6 24.9 %all-to-all-done.1 = bf16[32,128,64]{1,2,0:T(8,128)(2,1)S(1)} async-done(((bf16[32,128,64]{1,2,0:T(8,128)(2,1)}), bf16[32,128,64]{1,2,0:T(8,128)(2,1)S(1)}, u32[]{:S(2)}, u32[]{:S(2)}) %all-to-all-start.1) | async-done | bytes 524320 | tf_op jit(solution)/shard_map/all_to_all | solution.py:131
  144.5 24.1 %all-gather.5.cloned.1.call-done = bf16[512,2048]{1,0:T(8,128)(2,1)} async-done(((bf16[64,2048]{1,0:T(8,128)(2,1)}), bf16[512,2048]{1,0:T(8,128)(2,1)}) %all-gather.5.cloned.1.call-update) | async-done | bytes 2097168 | tf_op jit(solution)/shard_map/all_gather | solution.py:141
  168.7 2.5 convolution_dynamic-update-slice_fusion.1
  175.3 136.1 %all-reduce.4.cloned.1.call-done = (f32[512,512]{0,1:T(8,128)}, f32[512,1024]{1,0:T(8,128)}) async-done(((f32[512,512]{0,1:T(8,128)}, f32[512,1024]{1,0:T(8,128)}), (f32[512,512]{0,1:T(8,128)}, f32[512,1024]{1,0:T(8,128)})) %all-reduce.4.cloned.1.call-update) | async-done | bytes 3145744 | tf_op jit(solution)/shard_map/psum | solution.py:65
  311.4 2.4 select_add_fusion
  313.8 2.5 copy.70
  318.8 11.7 %cholesky.103 = f32[128,128]{1,0:T(8,128)S(1)} custom-call(f32[128,128]{1,0:T(8,128)S(1)} %cholesky.263), custom_call_target="Cholesky" | custom-call | tf_op jit(solution)/shard_map/jit(cholesky)/cholesky | solution.py:47
  330.6 9.8 %custom-call.32 = f32[1,128,128]{1,2,0:T(8,128)S(1)} custom-call(f32[1,128,128]{2,1,0:T(8,128)S(1)} %get-tuple-element.62), custom_call_target="InvertDiagBlocksLowerTriangular" | custom-call | tf_op jit(solution)/shard_map/jit(cholesky)/cholesky | solution.py:47
  343.1 12.1 %cholesky.215 = f32[128,128]{1,0:T(8,128)S(1)} custom-call(f32[128,128]{1,0:T(8,128)S(1)} %cholesky.267), custom_call_target="Cholesky" | custom-call | tf_op jit(solution)/shard_map/jit(cholesky)/cholesky | solution.py:47
  355.5 9.8 %custom-call.33 = f32[1,128,128]{1,2,0:T(8,128)S(1)} custom-call(f32[1,128,128]{2,1,0:T(8,128)S(1)} %get-tuple-element.60), custom_call_target="InvertDiagBlocksLowerTriangular" | custom-call | tf_op jit(solution)/shard_map/jit(cholesky)/cholesky | solution.py:47
  367.2 11.7 %cholesky.236 = f32[128,128]{1,0:T(8,128)S(1)} custom-call(f32[128,128]{1,0:T(8,128)S(1)} %cholesky.272), custom_call_target="Cholesky" | custom-call | tf_op jit(solution)/shard_map/jit(cholesky)/cholesky | solution.py:47
  379.0 9.8 %custom-call.34 = f32[1,128,128]{1,2,0:T(8,128)S(1)} custom-call(f32[1,128,128]{2,1,0:T(8,128)S(1)} %get-tuple-element.58), custom_call_target="InvertDiagBlocksLowerTriangular" | custom-call | tf_op jit(solution)/shard_map/jit(cholesky)/cholesky | solution.py:47
  390.5 11.9 %cholesky.253 = f32[128,128]{1,0:T(8,128)S(1)} custom-call(f32[128,128]{1,0:T(8,128)S(1)} %convolution_subtract_fusion.8), custom_call_target="Cholesky" | custom-call | tf_op jit(solution)/shard_map/jit(cholesky)/cholesky | solution.py:47
  405.1 3.2 broadcast_multiply_fusion
  412.4 14.5 %while.1 = (s32[]{:T(128)}, f32[512,512]{0,1:T(8,128)}, s32[4,2]{0,1:T(2,128)S(1)}, f32[4,128,128]{2,1,0:T(8,128)}, s32[]{:T(128)}) while((s32[]{:T(128)}, f32[512,512]{0,1:T(8,128)}, s32[4,2]{0,1:T(2,128)S(1)}, f32[4,128,128]{2,1,0:T(8,128)}, s32[]{:T(128)}) %tuple.40), condition=%wide.while_cond, body=%wide.while_body.sunk | while | flops 2 | bytes 393329 | solution.py:48
  413.1 2.2 dynamic-slice.7
  416.7 2.2 dynamic-slice.7
  420.4 2.2 dynamic-slice.7
  424.0 2.2 dynamic-slice.7
  426.9 40.1 %custom-call.35 = f32[4,128,128]{1,2,0:T(8,128)S(1)} custom-call(f32[4,128,128]{2,1,0:T(8,128)} %get-tuple-element.10), custom_call_target="InvertDiagBlocksLowerTriangular" | custom-call | tf_op jit(solution)/shard_map/triangular_solve | solution.py:48
  473.5 2.2 fusion.17
  484.0 2.0 fusion.14
  (136 shorter events, 61.8 us)
Async XLA Ops:
  7.2 75.3 %copy-start = (bf16[3,4,64,1024]{3,2,1,0:T(8,128)(2,1)S(1)}, bf16[3,4,64,1024]{3,2,1,0:T(8,128)(2,1)}, u32[]{:S(2)}) copy-start(bf16[3,4,64,1024]{3,2,1,0:T(8,128)(2,1)} %param.8) | copy-start | bytes 4718596
  7.2 66.8 %all-gather.3.cloned.1.call-start = ((), (), s32[]{:S(2)}) async-start(), calls=%async_computation.2 | async-start | bytes 3538944 | tf_op jit(solution)/shard_map/all_gather | solution.py:113
  9.1 159.4 %all-gather.5.cloned.1.call-start = ((), (), s32[]{:S(2)}) async-start(), calls=%async_computation.3 | async-start | bytes 2359296 | tf_op jit(solution)/shard_map/all_gather | solution.py:141
  80.4 2.4 copy-start.7
  85.7 0.8 copy-start.11
  85.7 0.8 copy-start.14
  85.8 0.9 copy-start.13
  86.9 2.2 copy-start.12
  114.3 54.4 %copy-start.9 = (bf16[64,2048]{1,0:T(8,128)(2,1)S(1)}, bf16[64,2048]{1,0:T(8,128)(2,1)}, u32[]{:S(2)}) copy-start(bf16[64,2048]{1,0:T(8,128)(2,1)} %reshape.250) | copy-start | bytes 786436
  116.7 27.7 %all-to-all-start.1 = ((bf16[32,128,64]{1,2,0:T(8,128)(2,1)}), bf16[32,128,64]{1,2,0:T(8,128)(2,1)S(1)}, u32[]{:S(2)}, u32[]{:S(2)}) async-start(bf16[32,128,64]{1,2,0:T(8,128)(2,1)} %bitcast.30), calls=%async_computation.1 | async-start | bytes 1048576 | tf_op jit(solution)/shard_map/all_to_all | solution.py:131
  119.3 192.1 %all-reduce.4.cloned.1.call-start = ((), (), s32[]{:S(2)}) async-start(), calls=%async_computation.4 | async-start | bytes 6291456 | tf_op jit(solution)/shard_map/psum | solution.py:65
  168.7 4.2 copy-start.1
  171.2 3.1 copy-start.6
  311.4 5.0 copy-start.5
  317.8 1.0 copy-start.8
  467.0 4.2 copy-start.3
  473.5 3.6 copy-start.4
  486.0 1.6 copy-start.2
  486.0 1.7 copy-start.10
Sparse Core Ops, SparseCore 0:
  10.8 63.1 all-gather.2
  113.4 55.1 all-gather.4
  174.8 136.5 all-reduce.3
where the time goes:
time: 504 us; the launch traced here: 496 us
  waiting for transfers between devices  243 us (48%)
  other arithmetic  141 us (28%)
  local copies, waits for them, and re-layouts  43.2 us (9%)
  matrix products  35.2 us (7%)
  between operations  17.1 us (3%)
  blocking collectives  13.8 us (3%)
    psum x1, waiting for transfers between devices, reduce_products(): return lax.psum((gram_part, cross_part), ('row', 'col'))  136 us
    another operation x15, other arithmetic, factor_panel(): lower_factor = jnp.linalg.cholesky(gram_matrix)  79.6 us
    all_gather x1, waiting for transfers between devices, per_device(): lax.all_gather(own_envs, 'col', axis=0, tiled=True)  57.7 us
    another operation x3, other arithmetic, factor_panel(): lax.linalg.triangular_solve(lower_factor, cross_sum / total_rows, left_si...  41.7 us
    all_to_all x1, waiting for transfers between devices, per_device(): lax.all_to_all(arrange_direct(trail_rows, row_count, col_count), ('row',...  24.9 us
    all_gather x1, waiting for transfers between devices, per_device(): segment = lax.all_gather(panel_own, 'col', axis=0, tiled=True)  24.1 us
    another operation x20, local copies, waits for them, and re-layouts  14.4 us
    all_to_all x1, blocking collectives, per_device(): lax.all_to_all(arrange_direct(panel_rows, row_count, col_count), ('row',...  13.8 us
  transfers between devices with their start and end apart: 4, of which 4 were waited for; matrix products, arithmetic and copies ran while one was open for 2% of the time, Pallas kernels for 0%

commit v1 on v0

--- a/solution.py
+++ b/solution.py
@@ -1,6 +1,8 @@
 import jax
 import jax.numpy as jnp
 from jax import lax
+from jax.experimental import pallas as pl
+from jax.experimental.pallas import tpu as pltpu
 from jax.sharding import PartitionSpec as P
 
 ridge_value = 0.1
@@ -40,29 +42,127 @@
     return jnp.take(slot_values, owner_order, axis=1)
 
 
+GROUP = 8
+BLOCK = 128
+
+
+def exact_dot(left_side, right_side, left_dim, right_dim):
+    return lax.dot_general(
+        left_side,
+        right_side,
+        (((left_dim,), (right_dim,)), ((), ())),
+        preferred_element_type=jnp.float32,
+        precision=lax.Precision.HIGHEST,
+    )
+
+
+def spread_row(values, row):
+    return jnp.broadcast_to(values[row : row + 1, :], values.shape)
+
+
+def eliminate_group(work_ref, group):
+    first = pl.multiple_of(group * GROUP, GROUP)
+    rows = work_ref[pl.ds(first, GROUP), :]
+    diag = rows[:, :BLOCK]
+    lanes = lax.broadcasted_iota(jnp.int32, (GROUP, BLOCK), 1)
+    sub = lax.broadcasted_iota(jnp.int32, (GROUP, BLOCK), 0)
+    sub_wide = lax.broadcasted_iota(jnp.int32, (GROUP, 2 * BLOCK), 0)
+    columns = [
+        jnp.broadcast_to(
+            jnp.sum(jnp.where(lanes == first + j, diag, 0.0), axis=1, keepdims=True),
+            (GROUP, BLOCK),
+        )
+        for j in range(GROUP)
+    ]
+    for j in range(GROUP):
+        pivot = spread_row(columns[j], j)
+        inverse = lax.rsqrt(pivot)
+        inverse = inverse * (1.5 - 0.5 * pivot * inverse * inverse)
+        scale = jnp.where(sub > j, columns[j] * inverse, 0.0)
+        for m in range(j + 1, GROUP):
+            columns[m] = columns[m] - scale * (spread_row(columns[m], j) * inverse)
+        both = jnp.concatenate([inverse, inverse], axis=1)
+        scale_both = jnp.concatenate([scale, scale], axis=1)
+        scaled = spread_row(rows, j) * both
+        rows = jnp.where(sub_wide == j, scaled, rows - scale_both * scaled)
+    work_ref[pl.ds(first, GROUP), :] = rows
+    later = jnp.where(lanes >= first + GROUP, rows[:, :BLOCK], 0.0)
+    work_ref[...] -= exact_dot(later, rows, 0, 0)
+
+
+def factor_kernel(
+    total_rows,
+    gram_ref,
+    cross_ref,
+    factor_ref,
+    coupled_ref,
+    high_ref,
+    low_ref,
+    field_ref,
+    work_ref,
+    inverse_ref,
+    weight_ref,
+):
+    size = gram_ref.shape[0]
+    blocks = size // BLOCK
+    row_ids = lax.broadcasted_iota(jnp.int32, (BLOCK, BLOCK), 0)
+    col_ids = lax.broadcasted_iota(jnp.int32, (BLOCK, BLOCK), 1)
+    unit = (row_ids == col_ids).astype(jnp.float32)
+    field_ref[:, :size] = gram_ref[...] / total_rows
+    field_ref[:, size:] = cross_ref[...] / total_rows
+    factor_ref[...] = jnp.zeros_like(factor_ref)
+    for b in range(blocks):
+        here = slice(b * BLOCK, (b + 1) * BLOCK)
+        after = (b + 1) * BLOCK
+        work_ref[:, :BLOCK] = field_ref[here, here] + ridge_value * unit
+        work_ref[:, BLOCK:] = unit
+
+        def step(group, carry):
+            eliminate_group(work_ref, group)
+            return carry
+
+        lax.fori_loop(0, BLOCK // GROUP, step, 0)
+        factor_ref[here, here] = jnp.where(col_ids >= row_ids, work_ref[:, :BLOCK], 0.0)
+        inverse = work_ref[:, BLOCK:]
+        inverse_ref[here, :] = inverse
+        row_rest = exact_dot(inverse, field_ref[here, after:], 1, 0)
+        field_ref[here, after:] = row_rest
+        if after < size:
+            factor_ref[here, after:] = row_rest[:, : size - after]
+            field_ref[after:, after:] -= exact_dot(row_rest[:, : size - after], row_rest, 0, 0)
+        coupled_ref[:, here] = row_rest[:, size - after :].T
+    for b in range(blocks - 1, -1, -1):
+        here = slice(b * BLOCK, (b + 1) * BLOCK)
+        after = (b + 1) * BLOCK
+        rest = field_ref[here, size:]
+        if after < size:
+            rest = rest - exact_dot(factor_ref[here, after:], weight_ref[after:, :], 1, 0)
+        weight_ref[here, :] = exact_dot(inverse_ref[here, :], rest, 0, 0)
+    weights = weight_ref[...]
+    high = weights.astype(jnp.bfloat16)
+    high_ref[...] = high
+    low_ref[...] = (weights - high.astype(jnp.float32)).astype(jnp.bfloat16)
+
+
 def factor_panel(gram_sum, cross_sum, total_rows):
-    gram_matrix = gram_sum / total_rows + ridge_value * jnp.eye(
-        gram_sum.shape[0], dtype=jnp.float32
-    )
-    lower_factor = jnp.linalg.cholesky(gram_matrix)
-    coupling = lax.linalg.triangular_solve(
-        lower_factor, cross_sum / total_rows, left_side=True, lower=True
-    )
-    weights = lax.linalg.triangular_solve(
-        lower_factor, coupling, left_side=True, lower=True, transpose_a=True
-    )
-    return (lower_factor.T, coupling, weights)
-
-
-def split_weights(weights):
-    weight_high = weights.astype(jnp.bfloat16)
-    held_high = lax.optimization_barrier(weight_high)
-    weight_low = (weights - held_high.astype(jnp.float32)).astype(jnp.bfloat16)
-    return (weight_high, weight_low)
-
-
-def reduce_products(gram_part, cross_part):
-    return lax.psum((gram_part, cross_part), ("row", "col"))
+    size, width = cross_sum.shape
+    return pl.pallas_call(
+        lambda *refs: factor_kernel(total_rows, *refs),
+        out_shape=(
+            jax.ShapeDtypeStruct((size, size), jnp.float32),
+            jax.ShapeDtypeStruct((width, size), jnp.float32),
+            jax.ShapeDtypeStruct((size, width), jnp.bfloat16),
+            jax.ShapeDtypeStruct((size, width), jnp.bfloat16),
+        ),
+        scratch_shapes=[
+            pltpu.VMEM((size, size + width), jnp.float32),
+            pltpu.VMEM((BLOCK, 2 * BLOCK), jnp.float32),
+            pltpu.VMEM((size, BLOCK), jnp.float32),
+            pltpu.VMEM((size, width), jnp.float32),
+        ],
+        compiler_params=pltpu.CompilerParams(vmem_limit_bytes=32 * 1024 * 1024),
+        name="factor_panel",
+    )(gram_sum, cross_sum)
 
 
 def contract_rows(left_side, right_side):
@@ -98,7 +198,6 @@
 ):
     row_count = lax.axis_size("row")
     col_count = lax.axis_size("col")
-    col_index = lax.axis_index("col")
     count_here = atom_counts[0]
     owner_here = owner_rows[0]
     slope_here = gradients.reshape(-1, gradients.shape[3])
@@ -139,31 +238,18 @@
     panel_own = restore_direct(received[0], row_count, col_count)
     trail_own = restore_direct(received[1], row_count, col_count)
     segment = lax.all_gather(panel_own, "col", axis=0, tiled=True)
-    columns = jnp.concatenate(
-        [contract_rows(segment, panel_own), contract_rows(segment, trail_own)], axis=1
-    )
-    gram_part = lax.dynamic_update_slice(
-        jnp.zeros((panel_total, panel_total), jnp.float32),
-        columns[:, :panel_width],
-        (0, col_index * panel_width),
-    )
-    cross_part = lax.dynamic_update_slice(
-        jnp.zeros((panel_total, trail_total), jnp.float32),
-        columns[:, panel_width:],
-        (0, col_index * trail_width),
-    )
-    gram_sum, cross_sum = reduce_products(gram_part, cross_part)
-    panel_factor, coupling, weights = factor_panel(gram_sum, cross_sum, total_rows)
-    coupling_own = lax.dynamic_slice_in_dim(coupling, col_index * trail_width, trail_width, 1)
-    weights_own = lax.dynamic_slice_in_dim(weights, col_index * trail_width, trail_width, 1)
-    weight_high, weight_low = split_weights(weights_own)
-    segment = lax.all_gather(panel_own, "col", axis=0, tiled=True)
+    own_rows = jnp.concatenate([panel_own, trail_own], axis=0)
+    products = lax.psum(contract_rows(own_rows, segment), "row")
+    gram_sum = lax.all_gather(products[:panel_width], "col", axis=0, tiled=True)
+    cross_sum = products[panel_width:].T
+    panel_factor, cross_factor, weight_high, weight_low = factor_panel(
+        gram_sum, cross_sum, total_rows
+    )
     trail_residual = (
         trail_own.astype(jnp.float32)
         - contract_cols(weight_high, segment)
         - contract_cols(weight_low, segment)
     )
-    cross_factor = coupling_own.T
     return (panel_factor, cross_factor, trail_residual)
 
 

time: 504 us -> 297 us (0.59); the launches traced: 496 us -> 296 us
  other arithmetic: 141 us -> 12.3 us
  waiting for transfers between devices: 243 us -> 179 us
  Pallas kernels: 0 us -> 38.4 us
  matrix products: 35.2 us -> 13.4 us
  local copies, waits for them, and re-layouts: 43.2 us -> 22.8 us
    another operation x19 -> x1, other arithmetic: 121 us -> 0.09 us  [the longest x15 79.6 us: factor_panel(): lower_factor = jnp.linalg.cholesky(gram_matrix)]
    psum x1, waiting for transfers between devices: 136 us -> 31.6 us  [per_device(): products = lax.psum(contract_rows(own_rows, segment), 'row')]
    all_gather x0 -> x1, waiting for transfers between devices: none -> 40.5 us  [per_device(): gram_sum = lax.all_gather(products[:panel_width], 'col', axis=0, tiled=True)]
    pallas_call x0 -> x1, Pallas kernels: none -> 38.4 us  [factor_panel(): pl.pallas_call(lambda *refs: factor_kernel(total_rows, *refs), out_shape=...]
    another operation x20 -> x0, matrix products: 22.8 us -> none  [the longest x7 9.25 us: factor_panel(): lax.linalg.triangular_solve(lower_factor, cross_sum / total_rows, left_si...]
    another operation x34 -> x0, local copies, waits for them, and re-layouts: 15.1 us -> none
  transfers between devices with their start and end apart: 4 -> 5, of which waited for: 4 -> 5; matrix products, arithmetic and copies ran while one was open for 2% -> 4% of each run, Pallas kernels for 0% -> 0%
where the time goes in v1:
time: 297 us; the launch traced here: 296 us
  waiting for transfers between devices  179 us (60%)
  Pallas kernels  38.4 us (13%)
  local copies, waits for them, and re-layouts  22.8 us (8%)
  between operations  14 us (5%)
  blocking collectives  13.8 us (5%)
  matrix products  13.4 us (5%)
  other arithmetic  12.3 us (4%)
    all_gather x1, waiting for transfers between devices, per_device(): lax.all_gather(own_envs, 'col', axis=0, tiled=True)  57.7 us
    all_gather x1, waiting for transfers between devices, per_device(): gram_sum = lax.all_gather(products[:panel_width], 'col', axis=0, tiled=True)  40.5 us
    pallas_call x1, Pallas kernels, factor_panel(): pl.pallas_call(lambda *refs: factor_kernel(total_rows, *refs), out_shape=...  38.4 us
    psum x1, waiting for transfers between devices, per_device(): products = lax.psum(contract_rows(own_rows, segment), 'row')  31.6 us
    all_to_all x1, waiting for transfers between devices, per_device(): lax.all_to_all(arrange_direct(trail_rows, row_count, col_count), ('row',...  24.8 us
    all_gather x1, waiting for transfers between devices, per_device(): segment = lax.all_gather(panel_own, 'col', axis=0, tiled=True)  24.1 us
    all_to_all x1, blocking collectives, per_device(): lax.all_to_all(arrange_direct(panel_rows, row_count, col_count), ('row',...  13.8 us
  transfers between devices with their start and end apart: 5, of which 5 were waited for; matrix products, arithmetic and copies ran while one was open for 4% of the time, Pallas kernels for 0%

profile of v1, /device:TPU:0, one launch (start us, length us, event | category | flops | bytes accessed | tf_op | source)
XLA Modules:
  0.0 296.3 jit_solution(5308385806870818830)
XLA Ops:
  7.2 1.9 pad_maximum_fusion
  10.5 1.0 compare_and_fusion
  12.3 0.8 select_reduce_fusion
  13.1 1.2 convert_bitcast_fusion
  16.3 57.7 %all-gather.4.cloned.1.call-done = bf16[1536,1024]{1,0:T(8,128)(2,1)} async-done(((bf16[192,1024]{1,0:T(8,128)(2,1)}), bf16[1536,1024]{1,0:T(8,128)(2,1)}) %all-gather.4.cloned.1.call-update) | async-done | bytes 3145744 | tf_op jit(solution)/shard_map/all_gather | solution.py:212
  74.0 3.6 %multiply_reduce_fusion.1 = (f32[1536,4]{0,1:T(4,128)}, f32[1536,64]{0,1:T(8,128)S(1)}) fusion(f32[4,16]{1,0:T(4,128)S(1)} %fusion.9, bf16[1536,1024]{1,0:T(8,128)(2,1)} %all-gather.4.cloned.1.call-done, bf16[64,1024]{1,0:T(8,128)(2,1)} %param.7), kind=kOutput, calls=%fused_computation.18 | convolution fusion | flops 201615360 | bytes 3694848 | tf_op jit(solution)/shard_map/dot_general | solution.py:16
  77.6 1.2 gather_fusion
  78.8 1.6 gather.13
  80.4 2.1 fusion.1
  82.8 2.9 multiply_reduce_fusion
  87.6 1.6 copy.67
  89.2 1.6 broadcast_select_fusion
  90.8 0.8 slice.20
  91.6 1.4 reshape.228
  93.1 13.8 %all_to_all.10 = bf16[32,2,2048]{2,1,0:T(2,128)(2,1)} all-to-all(bf16[32,2,2048]{2,1,0:T(2,128)(2,1)S(1)} %reshape.228), channel_id=1, replica_groups=mesh['row'=4,'col'=8] {'row','col'}, dimensions={0} | all-to-all | bytes 524288 | tf_op jit(solution)/shard_map/all_to_all | solution.py:223
  106.8 2.1 reshape.229
  109.0 2.2 copy.58
  111.2 2.2 reshape.207
  113.4 1.1 slice_bitcast_fusion
  114.5 2.4 copy.59
  116.9 2.6 all-to-all-start.1
  119.8 24.8 %all-to-all-done.1 = bf16[32,128,64]{1,2,0:T(8,128)(2,1)S(1)} async-done(((bf16[32,128,64]{1,2,0:T(8,128)(2,1)}), bf16[32,128,64]{1,2,0:T(8,128)(2,1)S(1)}, u32[]{:S(2)}, u32[]{:S(2)}) %all-to-all-start.1) | async-done | bytes 524320 | tf_op jit(solution)/shard_map/all_to_all | solution.py:230
  144.6 24.1 %all-gather.6.cloned.1.call-done = bf16[512,2048]{1,0:T(8,128)(2,1)} async-done(((bf16[64,2048]{1,0:T(8,128)(2,1)}), bf16[512,2048]{1,0:T(8,128)(2,1)}) %all-gather.6.cloned.1.call-update) | async-done | bytes 2097168 | tf_op jit(solution)/shard_map/all_gather | solution.py:240
  168.7 3.2 %fusion.2 = f32[192,512]{0,1:T(8,128)} fusion(bf16[512,2048]{1,0:T(8,128)(2,1)} %all-gather.6.cloned.1.call-done, bf16[128,2048]{0,1:T(8,128)(2,1)S(1)} %bitcast.59, bf16[64,2048]{0,1:T(8,128)(2,1)S(1)} %copy.61), kind=kOutput, calls=%fused_computation.11 | convolution fusion | flops 404226048 | bytes 3276800 | tf_op jit(solution)/shard_map/dot_general | solution.py:169
  172.2 31.6 %all-reduce.2.cloned.1.call-done = f32[192,512]{0,1:T(8,128)} async-done(((f32[192,512]{0,1:T(8,128)}), f32[192,512]{0,1:T(8,128)}) %all-reduce.2.cloned.1.call-update) | async-done | bytes 393232 | tf_op jit(solution)/shard_map/psum | solution.py:242
  203.8 1.0 slice.22
  204.8 0.8 copy.63
  206.0 40.5 %all-gather.8.cloned.1.call-done.refs_0_ = f32[512,512]{1,0:T(8,128)} async-done(((f32[64,512]{1,0:T(8,128)}), f32[512,512]{1,0:T(8,128)}) %all-gather.8.cloned.1.call-update) | async-done | bytes 1048592 | tf_op jit(solution)/shard_map/all_gather | solution.py:243
  246.5 1.2 copy-done.1
  247.7 38.4 %factor_panel.1 = (f32[512,512]{1,0:T(8,128)}, f32[128,512]{1,0:T(8,128)}, bf16[512,128]{1,0:T(8,128)(2,1)S(1)}, bf16[512,128]{1,0:T(8,128)(2,1)S(1)}) custom-call(f32[512,512]{1,0:T(8,128)S(1)} %copy-done.1, f32[512,128]{1,0:T(8,128)S(1)} %slice_bitcast_fusion.1.refs_1_), custom_call_target="tpu_custom_call" | custom-call | tf_op jit(solution)/shard_map/factor_panel/pallas_call | solution.py:149
  286.1 2.2 convolution_subtract_fusion.1
  288.3 1.4 convolution_subtract_fusion
  (51 shorter events, 7.3 us)
Async XLA Ops:
  7.2 75.3 %copy-start = (bf16[3,4,64,1024]{3,2,1,0:T(8,128)(2,1)S(1)}, bf16[3,4,64,1024]{3,2,1,0:T(8,128)(2,1)}, u32[]{:S(2)}) copy-start(bf16[3,4,64,1024]{3,2,1,0:T(8,128)(2,1)} %param.8) | copy-start | bytes 4718596
  7.2 66.8 %all-gather.4.cloned.1.call-start = ((), (), s32[]{:S(2)}) async-start(), calls=%async_computation.2 | async-start | bytes 3538944 | tf_op jit(solution)/shard_map/all_gather | solution.py:212
  9.1 159.6 %all-gather.6.cloned.1.call-start = ((), (), s32[]{:S(2)}) async-start(), calls=%async_computation.3 | async-start | bytes 2359296 | tf_op jit(solution)/shard_map/all_gather | solution.py:240
  80.4 2.4 copy-start.3
  85.9 0.7 copy-start.6
  85.9 0.7 copy-start.8
  85.9 0.8 copy-start.7
  87.6 1.6 copy-start.9
  114.5 5.1 %copy-start.4 = (bf16[64,2048]{1,0:T(8,128)(2,1)S(1)}, bf16[64,2048]{1,0:T(8,128)(2,1)}, u32[]{:S(2)}) copy-start(bf16[64,2048]{1,0:T(8,128)(2,1)} %reshape.207) | copy-start | bytes 786436
  116.9 27.7 %all-to-all-start.1 = ((bf16[32,128,64]{1,2,0:T(8,128)(2,1)}), bf16[32,128,64]{1,2,0:T(8,128)(2,1)S(1)}, u32[]{:S(2)}, u32[]{:S(2)}) async-start(bf16[32,128,64]{1,2,0:T(8,128)(2,1)} %bitcast.21), calls=%async_computation.1 | async-start | bytes 1048576 | tf_op jit(solution)/shard_map/all_to_all | solution.py:230
  119.5 84.3 %all-reduce.2.cloned.1.call-start = ((), (), s32[]{:S(2)}) async-start(), calls=%async_computation.4 | async-start | bytes 1048576 | tf_op jit(solution)/shard_map/psum | solution.py:242
  172.0 74.6 %all-gather.8.cloned.1.call-start = ((), (), s32[]{:S(2)}) async-start(), calls=%async_computation.5 | async-start | bytes 1179648 | tf_op jit(solution)/shard_map/all_gather | solution.py:243
  203.8 2.1 copy-start.5
  246.5 1.2 copy-start.1
  286.1 2.2 copy-start.2
Sparse Core Ops, SparseCore 0:
  10.8 63.1 all-gather.3
  113.5 55.1 all-gather.5
  172.1 31.6 all-reduce.1
  206.3 40.1 all-gather.7

commit v2 on v1

--- a/solution.py
+++ b/solution.py
@@ -165,6 +165,258 @@
     )(gram_sum, cross_sum)
 
 
+MESH = pl.DeviceIdType.MESH
+VMEM_SPEC = pl.BlockSpec(memory_space=pltpu.VMEM)
+
+
+def split_axis(count):
+    inner = 1
+    while 4 * inner * inner <= count:
+        inner *= 2
+    return count // inner, inner
+
+
+def here_and_peers(row_count, col_count):
+    row, col = lax.axis_index("row"), lax.axis_index("col")
+    outer, inner = split_axis(col_count)
+    core, lane = row % 2, col % inner
+    sibling = row + 1 - 2 * core
+    far = [(row, ((col // inner + d) % outer) * inner + lane) for d in range(1, outer)]
+    near = [(row, (col // inner) * inner + (lane + e) % inner) for e in range(1, inner)]
+    level = [((row + 2 * d) % row_count, col) for d in range(1, row_count // 2)]
+    return row, col, core, (sibling, col), far, near, level
+
+
+def greet(peers):
+    barrier = pltpu.get_barrier_semaphore()
+    for peer in peers:
+        pl.semaphore_signal(barrier, inc=1, device_id=peer, device_id_type=MESH)
+    pl.semaphore_wait(barrier, len(peers))
+
+
+def remote(source, target, send_sem, recv_sem, peer):
+    return pltpu.make_async_remote_copy(
+        src_ref=source,
+        dst_ref=target,
+        send_sem=send_sem,
+        recv_sem=recv_sem,
+        device_id=peer,
+        device_id_type=MESH,
+    )
+
+
+def relay(parts, count, place, far_sem, near_sem, side_sem, recv_sem):
+    row, col, core, sibling, far, near, _ = place
+    started = []
+
+    def send(part, block, sem, peer):
+        ref = parts(core, block)[part]
+        copy = remote(ref, ref, sem, recv_sem.at[part, core, block], peer)
+        copy.start()
+        started.append(copy)
+
+    def arrived(part, which, block):
+        ref = parts(which, block)[part]
+        remote(ref, ref, side_sem.at[part, 0], recv_sem.at[part, which, block], sibling).wait_recv()
+
+    def pass_on(part, block, step):
+        for e, peer in enumerate(near):
+            send(part, block, near_sem.at[part, step, e], peer)
+        send(part, block, side_sem.at[part, step], sibling)
+
+    for part in range(count):
+        for d, peer in enumerate(far):
+            send(part, col, far_sem.at[part, d], peer)
+    for part in range(count):
+        pass_on(part, col, 0)
+    outer, inner = len(far) + 1, len(near) + 1
+    for d in range(1, outer):
+        block = far[d - 1][1]
+        for part in range(count):
+            arrived(part, core, block)
+            pass_on(part, block, d)
+    home, lane = col // inner, col % inner
+    for d in range(outer):
+        for e in range(1, inner):
+            block = ((home + d) % outer) * inner + (lane + e) % inner
+            for part in range(count):
+                arrived(part, core, block)
+                send(part, block, side_sem.at[part, e * outer + d], sibling)
+    for block in range(outer * inner):
+        for part in range(count):
+            arrived(part, 1 - core, block)
+    for copy in started:
+        copy.wait_send()
+
+
+def relay_sems(count, col_count):
+    outer, inner = split_axis(col_count)
+    return [
+        pltpu.SemaphoreType.DMA((count, outer)),
+        pltpu.SemaphoreType.DMA((count, outer, inner)),
+        pltpu.SemaphoreType.DMA((count, col_count)),
+        pltpu.SemaphoreType.DMA((count, 2, col_count)),
+    ]
+
+
+def gather_kernel(
+    row_count, col_count, panel_ref, trail_ref, panels_ref, trails_ref, own_sem, *sems
+):
+    place = here_and_peers(row_count, col_count)
+    row, col, core, sibling, far, near, _ = place
+    panel_width, trail_width = panel_ref.shape[0], trail_ref.shape[0]
+    half = panel_ref.shape[1] // 2
+
+    def lanes(which):
+        return pl.ds(pl.multiple_of(which * half, half), half)
+
+    def parts(which, block):
+        panel_rows = pl.ds(pl.multiple_of(block * panel_width, panel_width), panel_width)
+        trail_rows = pl.ds(pl.multiple_of(block * trail_width, trail_width), trail_width)
+        return [panels_ref.at[panel_rows, lanes(which)], trails_ref.at[trail_rows, lanes(which)]]
+
+    own = parts(core, col)
+    copies = [
+        pltpu.make_async_copy(panel_ref.at[:, lanes(core)], own[0], own_sem.at[0]),
+        pltpu.make_async_copy(trail_ref.at[:, lanes(core)], own[1], own_sem.at[1]),
+    ]
+    for copy in copies:
+        copy.start()
+    greet([sibling, *far, *near])
+    for copy in copies:
+        copy.wait()
+    relay(parts, 2, place, *sems)
+
+
+def gather_environments(sparse_panel, sparse_trail, row_count, col_count):
+    depth = sparse_panel.shape[1]
+    return pl.pallas_call(
+        lambda *refs: gather_kernel(row_count, col_count, *refs),
+        out_shape=(
+            jax.ShapeDtypeStruct((col_count * sparse_panel.shape[0], depth), sparse_panel.dtype),
+            jax.ShapeDtypeStruct((col_count * sparse_trail.shape[0], depth), sparse_trail.dtype),
+        ),
+        in_specs=[VMEM_SPEC] * 2,
+        out_specs=(VMEM_SPEC, VMEM_SPEC),
+        scratch_shapes=[pltpu.SemaphoreType.DMA((2,)), *relay_sems(2, col_count)],
+        compiler_params=pltpu.CompilerParams(
+            collective_id=1, has_side_effects=True, vmem_limit_bytes=32 * 1024 * 1024
+        ),
+        name="gather_environments",
+    )(sparse_panel, sparse_trail)
+
+
+def sum_kernel(
+    row_count,
+    col_count,
+    gram_part,
+    cross_part,
+    gram_ref,
+    cross_ref,
+    side_ref,
+    level_ref,
+    side_send,
+    side_recv,
+    level_send,
+    level_recv,
+    cross_send,
+    cross_recv,
+    *sems,
+):
+    place = here_and_peers(row_count, col_count)
+    row, col, core, sibling, far, near, level = place
+    gram_half = gram_part.shape[0] // 2
+    cross_half = cross_part.shape[0] // 2
+    greet([sibling, *far, *near, *level])
+
+    def gram_rows(which):
+        return pl.ds(pl.multiple_of(which * gram_half, gram_half), gram_half)
+
+    def cross_rows(which):
+        return pl.ds(pl.multiple_of(which * cross_half, cross_half), cross_half)
+
+    to_side = [
+        remote(
+            gram_part.at[gram_rows(1 - core)],
+            side_ref.at[:gram_half],
+            side_send.at[0],
+            side_recv.at[0],
+            sibling,
+        ),
+        remote(
+            cross_part.at[cross_rows(1 - core)],
+            side_ref.at[gram_half:],
+            side_send.at[1],
+            side_recv.at[1],
+            sibling,
+        ),
+    ]
+    for copy in to_side:
+        copy.start()
+    for copy in to_side:
+        copy.wait()
+    floor = row // 2
+    level_ref[floor, :gram_half] = gram_part[gram_rows(core), :] + side_ref[:gram_half]
+    level_ref[floor, gram_half:] = cross_part[cross_rows(core), :] + side_ref[gram_half:]
+    to_level = []
+    for d, peer in enumerate(level):
+        mine = level_ref.at[floor]
+        copy = remote(mine, mine, level_send.at[d], level_recv.at[floor], peer)
+        copy.start()
+        to_level.append(copy)
+    for d, peer in enumerate(level):
+        other = peer[0] // 2
+        theirs = level_ref.at[other]
+        remote(theirs, theirs, level_send.at[d], level_recv.at[other], peer).wait_recv()
+    total = level_ref[0]
+    for other in range(1, row_count // 2):
+        total = total + level_ref[other]
+
+    def parts(which, block):
+        first = block * (2 * gram_half) + which * gram_half
+        return [gram_ref.at[pl.ds(pl.multiple_of(first, gram_half), gram_half)]]
+
+    parts(core, col)[0][...] = total[:gram_half]
+    cross_ref[cross_rows(core), :] = total[gram_half:]
+    mine = cross_ref.at[cross_rows(core)]
+    to_cross = remote(mine, mine, cross_send.at[0], cross_recv.at[0], sibling)
+    to_cross.start()
+    relay(parts, 1, place, *sems)
+    to_cross.wait()
+    for copy in to_level:
+        copy.wait_send()
+
+
+def sum_products(gram_part, cross_part, row_count, col_count):
+    width = gram_part.shape[1]
+    half = (gram_part.shape[0] + cross_part.shape[0]) // 2
+    levels = row_count // 2
+    return pl.pallas_call(
+        lambda *refs: sum_kernel(row_count, col_count, *refs),
+        out_shape=(
+            jax.ShapeDtypeStruct((gram_part.shape[0] * col_count, width), jnp.float32),
+            jax.ShapeDtypeStruct(cross_part.shape, jnp.float32),
+        ),
+        in_specs=[VMEM_SPEC] * 2,
+        out_specs=(VMEM_SPEC, VMEM_SPEC),
+        scratch_shapes=[
+            pltpu.VMEM((half, width), jnp.float32),
+            pltpu.VMEM((levels, half, width), jnp.float32),
+            pltpu.SemaphoreType.DMA((2,)),
+            pltpu.SemaphoreType.DMA((2,)),
+            pltpu.SemaphoreType.DMA((levels,)),
+            pltpu.SemaphoreType.DMA((levels,)),
+            pltpu.SemaphoreType.DMA((1,)),
+            pltpu.SemaphoreType.DMA((1,)),
+            *relay_sems(1, col_count),
+        ],
+        compiler_params=pltpu.CompilerParams(
+            collective_id=2, has_side_effects=True, vmem_limit_bytes=32 * 1024 * 1024
+        ),
+        name="sum_products",
+    )(gram_part, cross_part)
+
+
 def contract_rows(left_side, right_side):
     return lax.dot_general(
         left_side, right_side, (((1,), (1,)), ((), ())), preferred_element_type=jnp.float32
@@ -204,21 +456,16 @@
     panel_width = sparse_panel.shape[0]
     trail_width = sparse_trail.shape[0]
     panel_total = panel_width * col_count
-    trail_total = trail_width * col_count
     slot_count = 4 * neighbor_ids.shape[1]
     total_rows = row_count * row_count * col_count * slot_count
-    own_envs = jnp.concatenate([sparse_panel, sparse_trail], axis=0)
+    environments = jnp.concatenate(
+        gather_environments(sparse_panel, sparse_trail, row_count, col_count), axis=0
+    )
     kernel_rows = slot_rows(
-        lax.all_gather(own_envs, "col", axis=0, tiled=True),
-        descriptors,
-        slope_here,
-        count_here,
-        neighbor_ids,
-        owner_here,
-    )
-    blocks = kernel_rows.reshape(col_count, panel_width + trail_width, row_count, slot_count)
-    panel_rows = blocks[:, :panel_width].reshape(panel_total, row_count, slot_count)
-    trail_rows = blocks[:, panel_width:].reshape(trail_total, row_count, slot_count)
+        environments, descriptors, slope_here, count_here, neighbor_ids, owner_here
+    )
+    panel_rows = kernel_rows[:panel_total]
+    trail_rows = kernel_rows[panel_total:]
     received = (
         lax.all_to_all(
             arrange_direct(panel_rows, row_count, col_count),
@@ -238,10 +485,10 @@
     panel_own = restore_direct(received[0], row_count, col_count)
     trail_own = restore_direct(received[1], row_count, col_count)
     segment = lax.all_gather(panel_own, "col", axis=0, tiled=True)
-    own_rows = jnp.concatenate([panel_own, trail_own], axis=0)
-    products = lax.psum(contract_rows(own_rows, segment), "row")
-    gram_sum = lax.all_gather(products[:panel_width], "col", axis=0, tiled=True)
-    cross_sum = products[panel_width:].T
+    gram_sum, cross_sum = sum_products(
+        contract_rows(panel_own, segment), contract_rows(trail_own, segment), row_count, col_count
+    )
+    cross_sum = cross_sum.T
     panel_factor, cross_factor, weight_high, weight_low = factor_panel(
         gram_sum, cross_sum, total_rows
     )

time: 297 us -> 216 us (0.73)
  waiting for transfers between devices: 179 us -> 26.7 us
  Pallas kernels: 38.4 us -> 91.2 us
  blocking collectives: 13.8 us -> 44.8 us
  local copies, waits for them, and re-layouts: 22.8 us -> 16.1 us
  other arithmetic: 12.3 us -> 8.3 us
    all_gather x2 -> x0, waiting for transfers between devices: 98.2 us -> none  [the longest x1 57.7 us: per_device(): lax.all_gather(own_envs, 'col', axis=0, tiled=True)]
    pallas_call x0 -> x2, Pallas kernels: none -> 52.8 us  [the longest x1 31.1 us: gather_environments(): pl.pallas_call(lambda *refs: gather_kernel(row_count, col_count, *refs),...]
    psum x1 -> x0, waiting for transfers between devices: 31.6 us -> none  [per_device(): products = lax.psum(contract_rows(own_rows, segment), 'row')]
    all_to_all x0 -> x1, blocking collectives: none -> 25.7 us  [per_device(): lax.all_to_all(arrange_direct(trail_rows, row_count, col_count), ('row',...]
    all_to_all x1 -> x0, waiting for transfers between devices: 24.8 us -> none  [per_device(): lax.all_to_all(arrange_direct(trail_rows, row_count, col_count), ('row',...]
    all_to_all x1, blocking collectives: 13.8 us -> 19.1 us  [per_device(): lax.all_to_all(arrange_direct(panel_rows, row_count, col_count), ('row',...]
    transpose x2 -> x1, local copies, waits for them, and re-layouts: 3.44 us -> 0.12 us  [arrange_direct(): jnp.transpose(shaped, (2, 0, 1, 3))]
    concatenate x0 -> x1, local copies, waits for them, and re-layouts: none -> 3.11 us  [per_device(): jnp.concatenate(gather_environments(sparse_panel, sparse_trail, row_count...]
  transfers between devices with their start and end apart: 5 -> 1, of which waited for: 5 -> 1; matrix products, arithmetic and copies ran while one was open for 4% -> 1% of each run, Pallas kernels for 0% -> 0%
where the time goes in v2:
time: 216 us; the launch traced here: 215 us
  Pallas kernels  91.2 us (42%)
  blocking collectives  44.8 us (21%)
  waiting for transfers between devices  26.7 us (12%)
  local copies, waits for them, and re-layouts  16.1 us (7%)
  between operations  14.4 us (7%)
  matrix products  13.6 us (6%)
  other arithmetic  8.3 us (4%)
    pallas_call x1, Pallas kernels, factor_panel(): pl.pallas_call(lambda *refs: factor_kernel(total_rows, *refs), out_shape=...  38.4 us
    pallas_call x1, Pallas kernels, gather_environments(): pl.pallas_call(lambda *refs: gather_kernel(row_count, col_count, *refs),...  31.1 us
    all_gather x1, waiting for transfers between devices, per_device(): segment = lax.all_gather(panel_own, 'col', axis=0, tiled=True)  26.7 us
    all_to_all x1, blocking collectives, per_device(): lax.all_to_all(arrange_direct(trail_rows, row_count, col_count), ('row',...  25.7 us
    pallas_call x1, Pallas kernels, sum_products(): pl.pallas_call(lambda *refs: sum_kernel(row_count, col_count, *refs), out...  21.7 us
    all_to_all x1, blocking collectives, per_device(): lax.all_to_all(arrange_direct(panel_rows, row_count, col_count), ('row',...  19.1 us
    unnamed x30, local copies, waits for them, and re-layouts  5.48 us
  transfers between devices with their start and end apart: 1, of which 1 were waited for; matrix products, arithmetic and copies ran while one was open for 1% of the time, Pallas kernels for 0%

profile of v2, /device:TPU:0, one launch (start us, length us, event | category | flops | bytes accessed | tf_op | source)
XLA Modules:
  0.0 215.1 jit_solution(11884856224030667055)
XLA Ops:
  7.2 0.8 compare_select_fusion.3
  8.0 0.7 broadcast_compare_fusion
  8.7 0.7 fusion.5
  9.4 0.7 fusion.4
  10.1 1.2 convert_bitcast_fusion
  11.3 0.8 select_reduce_fusion
  12.1 0.5 fusion.6
  12.6 0.9 copy-done.2
  13.5 0.9 copy-done.3
  14.4 31.1 %gather_environments.1 = (bf16[512,1024]{1,0:T(8,128)(2,1)S(1)}, bf16[1024,1024]{1,0:T(8,128)(2,1)S(1)}) custom-call(bf16[64,1024]{1,0:T(8,128)(2,1)S(1)} %copy-done.3, bf16[128,1024]{1,0:T(8,128)(2,1)S(1)} %copy-done.2), custom_call_target="tpu_custom_call" | custom-call | tf_op jit(solution)/shard_map/gather_environments/pallas_call | solution.py:293
  45.6 1.4 copy-done.1
  46.9 1.0 constant_dynamic-update-slice_fusion.1
  48.5 3.1 %constant_dynamic-update-slice_fusion = bf16[1536,1024]{1,0:T(8,128)(2,1)} fusion(bf16[1536,1024]{1,0:T(8,128)(2,1)} %constant_dynamic-update-slice_fusion.1, bf16[1024,1024]{1,0:T(8,128)(2,1)} %copy-done.1), kind=kLoop, calls=%fused_computation.21 | loop fusion | bytes 4194304 | tf_op jit(solution)/shard_map/concatenate | solution.py:461
  51.6 3.6 %multiply_reduce_fusion.1 = (f32[1536,4]{0,1:T(4,128)}, f32[1536,64]{0,1:T(8,128)S(1)}) fusion(f32[4,16]{1,0:T(4,128)S(1)} %fusion.5, bf16[1536,1024]{1,0:T(8,128)(2,1)} %constant_dynamic-update-slice_fusion, bf16[64,1024]{1,0:T(8,128)(2,1)S(1)} %copy-done.8), kind=kOutput, calls=%fused_computation.12 | convolution fusion | flops 201615360 | bytes 3694848 | tf_op jit(solution)/shard_map/dot_general | solution.py:16
  55.2 1.2 gather_fusion
  56.4 1.6 gather.11
  58.1 2.1 fusion.1
  60.4 2.9 %multiply_reduce_fusion = f32[1536,3,4,16]{0,3,2,1:T(8,128)S(1)} fusion(bf16[3,4,4,16,1024]{4,3,2,1,0:T(8,128)(2,1)S(1)} %bitcast.64, bf16[1536,1024]{1,0:T(8,128)(2,1)S(1)} %copy-done.6, f32[1536,4,4,16]{0,3,2,1:T(8,128)S(1)} %fusion.1), kind=kOutput, calls=%fused_computation.2 | convolution fusion | flops 2417983488 | bytes 7471104 | tf_op jit(solution)/shard_map/dot_general | solution.py:19
  63.6 0.5 copy.48
  64.6 0.6 gather_fusion.1
  66.1 19.1 %all_to_all.10 = bf16[32,2,2048]{2,1,0:T(2,128)(2,1)S(1)} all-to-all(bf16[32,2,2048]{2,1,0:T(2,128)(2,1)S(1)} %reshape.234), channel_id=1, replica_groups=mesh['row'=4,'col'=8] {'row','col'}, dimensions={0} | all-to-all | bytes 524288 | tf_op jit(solution)/shard_map/all_to_all | solution.py:470
  85.5 0.4 copy.51
  85.9 1.2 reshape.212
  87.4 25.7 %all_to_all.11 = bf16[32,128,64]{1,2,0:T(8,128)(2,1)S(1)} all-to-all(bf16[32,128,64]{1,2,0:T(8,128)(2,1)S(1)} %bitcast.74), channel_id=1, replica_groups=mesh['row'=4,'col'=8] {'row','col'}, dimensions={0} | all-to-all | bytes 1048576 | tf_op jit(solution)/shard_map/all_to_all | solution.py:477
  113.1 1.0 copy.55
  114.1 26.7 %all-gather.2.cloned.1.call-done = bf16[512,2048]{1,0:T(8,128)(2,1)} async-done(((bf16[64,2048]{1,0:T(8,128)(2,1)}), bf16[512,2048]{1,0:T(8,128)(2,1)}) %all-gather.2.cloned.1.call-update) | async-done | bytes 2097168 | tf_op jit(solution)/shard_map/all_gather | solution.py:487
  140.8 2.6 %fusion.9.refs_1_ = f32[128,512]{1,0:T(8,128)S(1)} fusion(bf16[128,2048]{0,1:T(8,128)(2,1)S(1)} %bitcast.68, bf16[512,2048]{1,0:T(8,128)(2,1)} %all-gather.2.cloned.1.call-done), kind=kOutput, calls=%fused_computation.37 | convolution fusion | flops 268435456 | bytes 2883584 | tf_op jit(solution)/shard_map/dot_general | solution.py:421
  143.4 0.8 fusion.8.refs_0_
  144.2 21.7 %sum_products.1 = (f32[512,512]{1,0:T(8,128)S(1)}, f32[128,512]{1,0:T(8,128)S(1)}) custom-call(f32[64,512]{1,0:T(8,128)S(1)} %fusion.8.refs_0_, f32[128,512]{1,0:T(8,128)S(1)} %fusion.9.refs_1_), custom_call_target="tpu_custom_call" | custom-call | tf_op jit(solution)/shard_map/sum_products/pallas_call | solution.py:394
  166.1 38.4 %factor_panel.1 = (f32[512,512]{1,0:T(8,128)}, f32[128,512]{1,0:T(8,128)}, bf16[512,128]{1,0:T(8,128)(2,1)S(1)}, bf16[512,128]{1,0:T(8,128)(2,1)S(1)}) custom-call(f32[512,512]{1,0:T(8,128)S(1)} %get-tuple-element.13.refs_0_, f32[512,128]{1,0:T(8,128)S(1)} %bitcast.65), custom_call_target="tpu_custom_call" | custom-call | tf_op jit(solution)/shard_map/factor_panel/pallas_call | solution.py:149
  204.5 2.3 %convolution_subtract_fusion.1 = f32[128,2048]{1,0:T(8,128)S(1)} fusion(bf16[512,128]{1,0:T(8,128)(2,1)S(1)} %get-tuple-element.17, bf16[512,2048]{1,0:T(8,128)(2,1)} %all-gather.2.cloned.1.call-done, bf16[128,2048]{1,0:T(8,128)(2,1)} %copy.55), kind=kOutput, calls=%fused_computation.5 | convolution fusion | flops 268959744 | bytes 3801088 | tf_op jit(solution)/shard_map/dot_general | solution.py:427
  206.8 1.4 convolution_subtract_fusion
  (49 shorter events, 3.2 us)
Async XLA Ops:
  7.2 53.0 %copy-start = (bf16[3,4,64,1024]{3,2,1,0:T(8,128)(2,1)S(1)}, bf16[3,4,64,1024]{3,2,1,0:T(8,128)(2,1)}, u32[]{:S(2)}) copy-start(bf16[3,4,64,1024]{3,2,1,0:T(8,128)(2,1)} %param.8) | copy-start | bytes 4718596
  7.2 40.8 %copy-start.10 = (s32[4,16,4]{1,2,0:T(4,128)S(1)}, s32[4,16,4]{1,2,0:T(4,128)}, u32[]{:S(2)}) copy-start(s32[4,16,4]{1,2,0:T(4,128)} %param.13) | copy-start | bytes 3076
  7.2 133.7 %all-gather.2.cloned.1.call-start = ((), (), s32[]{:S(2)}) async-start(), calls=%async_computation.2 | async-start | bytes 2359296 | tf_op jit(solution)/shard_map/all_gather | solution.py:487
  12.6 0.9 copy-start.2
  13.5 0.9 copy-start.3
  45.6 1.4 copy-start.1
  48.5 3.1 %copy-start.8 = (bf16[64,1024]{1,0:T(8,128)(2,1)S(1)}, bf16[64,1024]{1,0:T(8,128)(2,1)}, u32[]{:S(2)}) copy-start(bf16[64,1024]{1,0:T(8,128)(2,1)} %param.7) | copy-start | bytes 393220
  58.1 2.4 %copy-start.6 = (bf16[1536,1024]{1,0:T(8,128)(2,1)S(1)}, bf16[1536,1024]{1,0:T(8,128)(2,1)}, u32[]{:S(2)}) copy-start(bf16[1536,1024]{1,0:T(8,128)(2,1)} %constant_dynamic-update-slice_fusion) | copy-start | bytes 9437188
  63.4 0.8 copy-start.12
  63.4 0.8 copy-start.9
  63.4 0.8 copy-start.11
  113.1 30.3 %copy-start.7 = (bf16[64,2048]{1,0:T(8,128)(2,1)S(1)}, bf16[64,2048]{1,0:T(8,128)(2,1)}, u32[]{:S(2)}) copy-start(bf16[64,2048]{1,0:T(8,128)(2,1)} %reshape.212) | copy-start | bytes 786436
  140.8 2.6 %copy-start.4 = (bf16[512,2048]{1,0:T(8,128)(2,1)S(1)}, bf16[512,2048]{1,0:T(8,128)(2,1)}, u32[]{:S(2)}) copy-start(bf16[512,2048]{1,0:T(8,128)(2,1)} %all-gather.2.cloned.1.call-done) | copy-start | bytes 6291460
  204.4 2.4 %copy-start.5 = (bf16[512,2048]{1,0:T(8,128)(2,1)S(1)}, bf16[512,2048]{1,0:T(8,128)(2,1)}, u32[]{:S(2)}) copy-start(bf16[512,2048]{1,0:T(8,128)(2,1)} %all-gather.2.cloned.1.call-done) | copy-start | bytes 6291460
Sparse Core Ops, SparseCore 0:
  87.2 53.5 all-gather.1

commit v3 on v2

--- a/solution.py
+++ b/solution.py
@@ -6,44 +6,6 @@
 from jax.sharding import PartitionSpec as P
 
 ridge_value = 0.1
-
-
-def slot_rows(environments, desc_here, slope_here, count_here, neighbor_here, owner_here):
-    struct_count = count_here.shape[0]
-    atom_slots = neighbor_here.shape[1]
-    neighbor_count = neighbor_here.shape[2]
-    env_count = environments.shape[0]
-    correlation = lax.dot_general(
-        environments, desc_here, (((1,), (1,)), ((), ())), preferred_element_type=jnp.float32
-    )
-    slope_dots = lax.dot_general(
-        environments, slope_here, (((1,), (1,)), ((), ())), preferred_element_type=jnp.float32
-    )
-    slope_dots = slope_dots.reshape(env_count, 3, neighbor_count, struct_count, atom_slots)
-    slot_index = jnp.arange(atom_slots, dtype=jnp.int32)
-    live_mask = (slot_index[None, :] < count_here[:, None]).astype(jnp.float32)
-    squares = (correlation * correlation).reshape(env_count, struct_count, atom_slots)
-    energy = jnp.sum(squares * live_mask[None], axis=2) / count_here.astype(jnp.float32)[None, :]
-    partner = neighbor_here % count_here[:, None, None]
-    struct_index = jnp.arange(struct_count, dtype=jnp.int32)
-    flat_index = (struct_index[:, None, None] * atom_slots + partner).reshape(-1)
-    picked = jnp.take(correlation, flat_index, axis=1).reshape(
-        env_count, struct_count, atom_slots, neighbor_count
-    )
-    picked = jnp.transpose(picked, (0, 3, 1, 2))
-    forces = -2.0 * jnp.sum(picked[:, None] * slope_dots, axis=2) * live_mask[None, None]
-    forces = jnp.transpose(forces, (0, 2, 3, 1)).reshape(env_count, struct_count, 3 * atom_slots)
-    padding = jnp.zeros((env_count, struct_count, atom_slots - 1), jnp.float32)
-    slot_values = jnp.concatenate([energy[:, :, None], forces, padding], axis=2).astype(
-        jnp.bfloat16
-    )
-    chosen = (owner_here[None, :] == struct_index[:, None]).astype(jnp.int32)
-    owner_order = jnp.sum(struct_index[None, :] * chosen, axis=1)
-    return jnp.take(slot_values, owner_order, axis=1)
-
-
-GROUP = 8
-BLOCK = 128
 
 
 def exact_dot(left_side, right_side, left_dim, right_dim):
@@ -54,6 +16,51 @@
         preferred_element_type=jnp.float32,
         precision=lax.Precision.HIGHEST,
     )
+
+
+def slot_rows(environments, desc_here, slope_here, count_here, neighbor_here, owner_here):
+    struct_count, atom_slots, neighbor_count = neighbor_here.shape
+    env_count = environments.shape[0]
+    atoms = struct_count * atom_slots
+    correlation = contract_rows(desc_here, environments)
+    slope_dots = contract_rows(slope_here, environments)
+    slope_dots = slope_dots.reshape(3, neighbor_count, atoms, env_count)
+    slot_index = jnp.arange(atom_slots, dtype=jnp.int32)
+    live_mask = (slot_index[None, :] < count_here[:, None]).astype(jnp.float32)
+    squares = (correlation * correlation).reshape(struct_count, atom_slots, env_count)
+    energy = jnp.sum(squares * live_mask[:, :, None], axis=1) / count_here.astype(jnp.float32)[
+        :, None
+    ]
+    partner = neighbor_here % count_here[:, None, None]
+    struct_index = jnp.arange(struct_count, dtype=jnp.int32)
+    flat_index = struct_index[:, None, None] * atom_slots + partner
+    flat_index = jnp.transpose(flat_index.reshape(atoms, neighbor_count))
+    atom_index = jnp.arange(atoms, dtype=jnp.int32)
+    chooser = jnp.where(
+        flat_index[:, :, None] == atom_index, -2.0 * live_mask.reshape(1, atoms, 1), 0.0
+    )
+    picked = exact_dot(chooser.reshape(neighbor_count * atoms, atoms), correlation, 1, 0)
+    picked = picked.reshape(1, neighbor_count, atoms, env_count)
+    forces = jnp.sum(picked * slope_dots, axis=1).reshape(3 * atoms, env_count)
+    values = jnp.concatenate(
+        [energy.astype(jnp.bfloat16), forces.astype(jnp.bfloat16)], axis=0
+    )
+    chosen = (owner_here[None, :] == struct_index[:, None]).astype(jnp.int32)
+    owner_order = jnp.sum(struct_index[None, :] * chosen, axis=1)[:, None]
+    slot = jnp.arange(4 * atom_slots, dtype=jnp.int32)[None, :]
+    atom, axis = (slot - 1) // 3, (slot - 1) % 3
+    source = struct_count + axis * atoms + owner_order * atom_slots + atom
+    source = jnp.where(slot <= 3 * atom_slots, source, -1)
+    source = jnp.where(slot == 0, owner_order, source).reshape(-1)
+    value_index = jnp.arange(values.shape[0], dtype=jnp.int32)
+    placing = (source[:, None] == value_index[None, :]).astype(jnp.bfloat16)
+    return lax.dot_general(
+        placing, values, (((1,), (0,)), ((), ())), preferred_element_type=jnp.float32
+    ).astype(jnp.bfloat16)
+
+
+GROUP = 8
+BLOCK = 128
 
 
 def spread_row(values, row):
@@ -260,7 +267,7 @@
 
 
 def gather_kernel(
-    row_count, col_count, panel_ref, trail_ref, panels_ref, trails_ref, own_sem, *sems
+    row_count, col_count, panel_ref, trail_ref, all_ref, own_sem, *sems
 ):
     place = here_and_peers(row_count, col_count)
     row, col, core, sibling, far, near, _ = place
@@ -272,8 +279,9 @@
 
     def parts(which, block):
         panel_rows = pl.ds(pl.multiple_of(block * panel_width, panel_width), panel_width)
-        trail_rows = pl.ds(pl.multiple_of(block * trail_width, trail_width), trail_width)
-        return [panels_ref.at[panel_rows, lanes(which)], trails_ref.at[trail_rows, lanes(which)]]
+        first = col_count * panel_width + block * trail_width
+        trail_rows = pl.ds(pl.multiple_of(first, panel_width), trail_width)
+        return [all_ref.at[panel_rows, lanes(which)], all_ref.at[trail_rows, lanes(which)]]
 
     own = parts(core, col)
     copies = [
@@ -290,20 +298,152 @@
 
 def gather_environments(sparse_panel, sparse_trail, row_count, col_count):
     depth = sparse_panel.shape[1]
+    width = sparse_panel.shape[0] + sparse_trail.shape[0]
     return pl.pallas_call(
         lambda *refs: gather_kernel(row_count, col_count, *refs),
-        out_shape=(
-            jax.ShapeDtypeStruct((col_count * sparse_panel.shape[0], depth), sparse_panel.dtype),
-            jax.ShapeDtypeStruct((col_count * sparse_trail.shape[0], depth), sparse_trail.dtype),
-        ),
+        out_shape=jax.ShapeDtypeStruct((col_count * width, depth), sparse_panel.dtype),
         in_specs=[VMEM_SPEC] * 2,
-        out_specs=(VMEM_SPEC, VMEM_SPEC),
+        out_specs=VMEM_SPEC,
         scratch_shapes=[pltpu.SemaphoreType.DMA((2,)), *relay_sems(2, col_count)],
         compiler_params=pltpu.CompilerParams(
             collective_id=1, has_side_effects=True, vmem_limit_bytes=32 * 1024 * 1024
         ),
         name="gather_environments",
     )(sparse_panel, sparse_trail)
+
+
+def exchange_kernel(
+    row_count,
+    col_count,
+    rows_ref,
+    panel_ref,
+    trail_ref,
+    held_ref,
+    own_sem,
+    row_send,
+    row_recv,
+    far_send,
+    near_send,
+    panel_recv,
+    trail_send,
+    trail_recv,
+):
+    row, col, core, sibling, far, near, _ = here_and_peers(row_count, col_count)
+    panel_total = panel_ref.shape[1]
+    trail_width = trail_ref.shape[1]
+    slots = rows_ref.shape[0] // row_count
+    wide = held_ref.shape[0]
+    groups = [(row + d) % row_count for d in range(1, row_count)]
+    others = [(col + d) % col_count for d in range(1, col_count)]
+    sides = [slice(0, panel_total), slice(panel_total, rows_ref.shape[1])]
+
+    def slot_range(group):
+        return pl.ds(pl.multiple_of(group * slots, slots), slots)
+
+    def wide_range(block):
+        return pl.ds(pl.multiple_of(block * wide, wide), wide)
+
+    own = pltpu.make_async_copy(
+        rows_ref.at[slot_range(row)], held_ref.at[slot_range(row)], own_sem.at[0]
+    )
+    own.start()
+    greet([(group, col) for group in groups] + [(row, other) for other in others])
+    started = []
+
+    def send(source, target, send_sem, recv_sem, peer):
+        copy = remote(source, target, send_sem, recv_sem, peer)
+        copy.start()
+        started.append(copy)
+
+    def arrived(target, recv_sem):
+        remote(target, target, row_send.at[0, 0], recv_sem, sibling).wait_recv()
+
+    for side, lanes in enumerate(sides):
+        for d, group in enumerate(groups):
+            send(
+                rows_ref.at[slot_range(group), lanes],
+                held_ref.at[slot_range(row), lanes],
+                row_send.at[side, d],
+                row_recv.at[side, row],
+                (group, col),
+            )
+    own.wait()
+    for group in groups:
+        arrived(held_ref.at[slot_range(group), sides[0]], row_recv.at[0, group])
+    mine = held_ref.at[:, sides[0]]
+    for d, peer in enumerate(far):
+        send(mine, panel_ref.at[wide_range(col)], far_send.at[d], panel_recv.at[col], peer)
+    for e, peer in enumerate(near):
+        send(mine, panel_ref.at[wide_range(col)], near_send.at[0, e], panel_recv.at[col], peer)
+    keep = pltpu.make_async_copy(mine, panel_ref.at[wide_range(col)], own_sem.at[1])
+    keep.start()
+    for group in groups:
+        arrived(held_ref.at[slot_range(group), sides[1]], row_recv.at[1, group])
+
+    def trail_lanes(block):
+        first = panel_total + block * trail_width
+        return pl.ds(pl.multiple_of(first, trail_width), trail_width)
+
+    for d, other in enumerate(others):
+        send(
+            held_ref.at[:, trail_lanes(other)],
+            trail_ref.at[wide_range(col)],
+            trail_send.at[d],
+            trail_recv.at[col],
+            (row, other),
+        )
+    keep_trail = pltpu.make_async_copy(
+        held_ref.at[:, trail_lanes(col)], trail_ref.at[wide_range(col)], own_sem.at[2]
+    )
+    keep_trail.start()
+    outer, inner = len(far) + 1, len(near) + 1
+    for d in range(1, outer):
+        block = far[d - 1][1]
+        ref = panel_ref.at[wide_range(block)]
+        arrived(ref, panel_recv.at[block])
+        for e, peer in enumerate(near):
+            send(ref, ref, near_send.at[d, e], panel_recv.at[block], peer)
+    home, lane = col // inner, col % inner
+    for d in range(outer):
+        for e in range(1, inner):
+            block = ((home + d) % outer) * inner + (lane + e) % inner
+            arrived(panel_ref.at[wide_range(block)], panel_recv.at[block])
+    for other in others:
+        arrived(trail_ref.at[wide_range(other)], trail_recv.at[other])
+    keep.wait()
+    keep_trail.wait()
+    for copy in started:
+        copy.wait_send()
+
+
+def exchange_rows(kernel_rows, panel_total, row_count, col_count):
+    total, env_count = kernel_rows.shape
+    trail_width = (env_count - panel_total) // col_count
+    outer, inner = split_axis(col_count)
+    return pl.pallas_call(
+        lambda *refs: exchange_kernel(row_count, col_count, *refs),
+        out_shape=(
+            jax.ShapeDtypeStruct((total * col_count, panel_total), kernel_rows.dtype),
+            jax.ShapeDtypeStruct((total * col_count, trail_width), kernel_rows.dtype),
+        ),
+        in_specs=[VMEM_SPEC],
+        out_specs=(VMEM_SPEC, VMEM_SPEC),
+        scratch_shapes=[
+            pltpu.VMEM((total, env_count), kernel_rows.dtype),
+            pltpu.SemaphoreType.DMA((3,)),
+            pltpu.SemaphoreType.DMA((2, row_count)),
+            pltpu.SemaphoreType.DMA((2, row_count)),
+            pltpu.SemaphoreType.DMA((outer,)),
+            pltpu.SemaphoreType.DMA((outer, inner)),
+            pltpu.SemaphoreType.DMA((col_count,)),
+            pltpu.SemaphoreType.DMA((col_count,)),
+            pltpu.SemaphoreType.DMA((col_count,)),
+        ],
+        compiler_params=pltpu.CompilerParams(
+            collective_id=3, has_side_effects=True, vmem_limit_bytes=40 * 1024 * 1024
+        ),
+        name="exchange_rows",
+    )(kernel_rows)
 
 
 def sum_kernel(
@@ -429,19 +569,9 @@
     )
 
 
-def arrange_direct(block_rows, row_count, col_count):
-    env_width = block_rows.shape[0] // col_count
-    slot_count = block_rows.shape[2]
-    shaped = block_rows.reshape(col_count, env_width, row_count, slot_count)
-    return jnp.transpose(shaped, (2, 0, 1, 3)).reshape(row_count * col_count, env_width, slot_count)
-
-
-def restore_direct(block_rows, row_count, col_count):
-    env_width = block_rows.shape[1]
-    slot_count = block_rows.shape[2]
-    shaped = block_rows.reshape(row_count, col_count, env_width, slot_count)
-    return jnp.transpose(shaped, (2, 1, 0, 3)).reshape(
-        env_width, row_count * col_count * slot_count
+def project(weights, segment):
+    return lax.dot_general(
+        weights, segment, (((0,), (1,)), ((), ())), preferred_element_type=jnp.float32
     )
 
 
@@ -454,48 +584,27 @@
     owner_here = owner_rows[0]
     slope_here = gradients.reshape(-1, gradients.shape[3])
     panel_width = sparse_panel.shape[0]
-    trail_width = sparse_trail.shape[0]
     panel_total = panel_width * col_count
     slot_count = 4 * neighbor_ids.shape[1]
     total_rows = row_count * row_count * col_count * slot_count
-    environments = jnp.concatenate(
-        gather_environments(sparse_panel, sparse_trail, row_count, col_count), axis=0
-    )
+    environments = gather_environments(sparse_panel, sparse_trail, row_count, col_count)
     kernel_rows = slot_rows(
         environments, descriptors, slope_here, count_here, neighbor_ids, owner_here
     )
-    panel_rows = kernel_rows[:panel_total]
-    trail_rows = kernel_rows[panel_total:]
-    received = (
-        lax.all_to_all(
-            arrange_direct(panel_rows, row_count, col_count),
-            ("row", "col"),
-            split_axis=0,
-            concat_axis=0,
-            tiled=True,
-        ),
-        lax.all_to_all(
-            arrange_direct(trail_rows, row_count, col_count),
-            ("row", "col"),
-            split_axis=0,
-            concat_axis=0,
-            tiled=True,
-        ),
-    )
-    panel_own = restore_direct(received[0], row_count, col_count)
-    trail_own = restore_direct(received[1], row_count, col_count)
-    segment = lax.all_gather(panel_own, "col", axis=0, tiled=True)
+    segment, trail_own = exchange_rows(kernel_rows, panel_total, row_count, col_count)
+    first = lax.axis_index("col") * panel_width
+    panel_own = lax.dynamic_slice_in_dim(segment, first, panel_width, 1)
     gram_sum, cross_sum = sum_products(
-        contract_rows(panel_own, segment), contract_rows(trail_own, segment), row_count, col_count
+        contract_cols(panel_own, segment), contract_cols(trail_own, segment), row_count, col_count
     )
     cross_sum = cross_sum.T
     panel_factor, cross_factor, weight_high, weight_low = factor_panel(
         gram_sum, cross_sum, total_rows
     )
     trail_residual = (
-        trail_own.astype(jnp.float32)
-        - contract_cols(weight_high, segment)
-        - contract_cols(weight_low, segment)
+        trail_own.T.astype(jnp.float32)
+        - project(weight_high, segment)
+        - project(weight_low, segment)
     )
     return (panel_factor, cross_factor, trail_residual)
 

time: 216 us -> 178 us (0.82)
  Pallas kernels: 91.2 us -> 153 us
  blocking collectives: 44.8 us -> 0 us
  waiting for transfers between devices: 26.7 us -> 0 us
  between operations: 14.4 us -> 0.84 us
  local copies, waits for them, and re-layouts: 16.1 us -> 6.67 us
  other arithmetic: 8.3 us -> 3.69 us
    pallas_call x0 -> x1, Pallas kernels: none -> 48.5 us  [exchange_rows(): pl.pallas_call(lambda *refs: exchange_kernel(row_count, col_count, *refs)...]
    all_to_all x2 -> x0, blocking collectives: 44.8 us -> none  [the longest x1 25.7 us: per_device(): lax.all_to_all(arrange_direct(trail_rows, row_count, col_count), ('row',...]
    all_gather x1 -> x0, waiting for transfers between devices: 26.7 us -> none  [per_device(): segment = lax.all_gather(panel_own, 'col', axis=0, tiled=True)]
    pallas_call x1, Pallas kernels: 21.7 us -> 35.3 us  [sum_products(): pl.pallas_call(lambda *refs: sum_kernel(row_count, col_count, *refs), out...]
    gather x3 -> x0, local copies, waits for them, and re-layouts: 3.46 us -> none  [the longest x2 2.86 us: slot_rows(): jnp.take(correlation, flat_index, axis=1)]
    concatenate x2 -> x0, local copies, waits for them, and re-layouts: 3.18 us -> none  [the longest x1 3.11 us: per_device(): jnp.concatenate(gather_environments(sparse_panel, sparse_trail, row_count...]
    reshape x5 -> x1, local copies, waits for them, and re-layouts: 2.66 us -> 0.08 us  [slot_rows(): flat_index = jnp.transpose(flat_index.reshape(atoms, neighbor_count))]
    reduce_sum x1 -> x2, other arithmetic: 0.77 us -> 3.09 us  [the longest x1 2.97 us: slot_rows(): forces = jnp.sum(picked * slope_dots, axis=1).reshape(3 * atoms, env_count)]
  transfers between devices with their start and end apart: 1 -> 0, of which waited for: 1 -> 0; matrix products, arithmetic and copies ran while one was open for 1% -> 0% of each run, Pallas kernels for 0% -> 0%
where the time goes in v3:
time: 178 us
  Pallas kernels  153 us (86%)
  matrix products  13.4 us (8%)
  local copies, waits for them, and re-layouts  6.67 us (4%)
  other arithmetic  3.69 us (2%)
    pallas_call x1, Pallas kernels, exchange_rows(): pl.pallas_call(lambda *refs: exchange_kernel(row_count, col_count, *refs)...  48.5 us
    pallas_call x1, Pallas kernels, factor_panel(): pl.pallas_call(lambda *refs: factor_kernel(total_rows, *refs), out_shape=...  38.5 us
    pallas_call x1, Pallas kernels, sum_products(): pl.pallas_call(lambda *refs: sum_kernel(row_count, col_count, *refs), out...  35.3 us
    pallas_call x1, Pallas kernels, gather_environments(): pl.pallas_call(lambda *refs: gather_kernel(row_count, col_count, *refs),...  31.1 us
    dot_general x2, matrix products, contract_rows(): lax.dot_general(left_side, right_side, (((1,), (1,)), ((), ())), preferre...  5.38 us
    unnamed x23, local copies, waits for them, and re-layouts  5.34 us

profile of v3, /device:TPU:0, one launch (start us, length us, event | category | flops | bytes accessed | tf_op | source)
XLA Modules:
  0.0 178.1 jit_solution(5899566199184978199)
XLA Ops:
  0.6 0.0 copy-start
  0.7 1.1 copy-done.4
  1.7 0.9 copy-done.6
  2.6 31.1 %gather_environments.1 = bf16[1536,1024]{1,0:T(8,128)(2,1)S(1)} custom-call(bf16[64,1024]{1,0:T(8,128)(2,1)S(1)} %copy-done.6, bf16[128,1024]{1,0:T(8,128)(2,1)S(1)} %copy-done.4), custom_call_target="tpu_custom_call" | custom-call | tf_op jit(solution)/shard_map/gather_environments/pallas_call | solution.py:302
  33.8 0.0 copy-start.9
  33.8 0.0 copy-start.7
  33.8 4.3 %fusion.21 = f32[1536,768]{0,1:T(8,128)} fusion(bf16[1536,1024]{1,0:T(8,128)(2,1)S(1)} %gather_environments.1, bf16[768,1024]{1,0:T(8,128)(2,1)S(1)} %bitcast.35), kind=kOutput, calls=%fused_computation.44 | convolution fusion | flops 2415919104 | bytes 9437184 | tf_op jit(solution)/shard_map/dot_general | solution.py:561
  38.1 0.1 fusion.14
  38.1 1.1 multiply_reduce_fusion.1
  39.2 0.1 fusion.13
  39.3 0.1 mul.82
  39.4 0.3 fusion.12
  39.7 0.1 reshape.221
  39.8 1.4 fusion.5
  41.2 0.0 copy-start.10
  41.2 3.0 %multiply_reduce_fusion = bf16[3,64,1536]{2,1,0:T(8,128)(2,1)S(1)} fusion(f32[3,4,64,1536]{3,2,1,0:T(8,128)} %bitcast.37, f32[4,64,1536]{2,1,0:T(8,128)S(1)} %fusion.5), kind=kLoop, calls=%fused_computation | loop fusion | flops 2064384 | bytes 6881280 | tf_op jit(solution)/shard_map/reduce_sum | solution.py:44
  44.2 0.1 divide_convert_fusion
  44.3 0.1 select_reduce_fusion
  44.5 0.1 select_select_fusion
  44.5 0.1 select_n.75
  44.6 0.4 convolution_convert_fusion.refs_0_
  45.1 48.5 %exchange_rows.1 = (bf16[2048,512]{1,0:T(8,128)(2,1)S(1)}, bf16[2048,128]{1,0:T(8,128)(2,1)S(1)}) custom-call(bf16[256,1536]{1,0:T(8,128)(2,1)S(1)} %convolution_convert_fusion.refs_0_), custom_call_target="tpu_custom_call" | custom-call | tf_op jit(solution)/shard_map/exchange_rows/pallas_call | solution.py:423
  93.6 1.3 copy-done.1
  94.9 2.6 %fusion.3.refs_0_ = f32[64,512]{1,0:T(8,128)S(1)} fusion(bf16[2048,512]{1,0:T(8,128)(2,1)} %copy-done.1, s32[]{:T(128)S(6)} %select_n.79), kind=kOutput, calls=%fused_computation.7 | convolution fusion | flops 134217728 | bytes 2752516 | tf_op jit(solution)/shard_map/dot_general | solution.py:567
  97.5 0.5 fusion.22.refs_1_
  98.0 35.3 %sum_products.1 = (f32[512,512]{1,0:T(8,128)S(1)}, f32[128,512]{1,0:T(8,128)S(1)}) custom-call(f32[64,512]{1,0:T(8,128)S(1)} %fusion.3.refs_0_, f32[128,512]{1,0:T(8,128)S(1)} %fusion.22.refs_1_), custom_call_target="tpu_custom_call" | custom-call | tf_op jit(solution)/shard_map/sum_products/pallas_call | solution.py:534
  133.3 0.7 copy-done.5
  134.0 1.1 copy.20
  135.1 38.5 %factor_panel.1 = (f32[512,512]{1,0:T(8,128)}, f32[128,512]{1,0:T(8,128)}, bf16[512,128]{1,0:T(8,128)(2,1)S(1)}, bf16[512,128]{1,0:T(8,128)(2,1)S(1)}) custom-call(f32[512,512]{1,0:T(8,128)S(1)} %get-tuple-element.13.refs_0_, f32[512,128]{1,0:T(8,128)S(1)} %bitcast.36), custom_call_target="tpu_custom_call" | custom-call | tf_op jit(solution)/shard_map/factor_panel/pallas_call | solution.py:156
  173.6 2.4 %convolution_subtract_fusion.1 = f32[128,2048]{0,1:T(8,128)S(1)} fusion(bf16[2048,512]{1,0:T(8,128)(2,1)} %copy-done.1, bf16[512,128]{1,0:T(8,128)(2,1)S(1)} %get-tuple-element.17, bf16[2048,128]{1,0:T(8,128)(2,1)S(1)} %get-tuple-element.12), kind=kOutput, calls=%fused_computation.3 | convolution fusion | flops 268959744 | bytes 3801088 | tf_op jit(solution)/shard_map/dot_general | solution.py:573
  176.1 0.7 convolution_subtract_fusion
  176.8 1.3 copy.23
  (21 shorter events, 0.1 us)
Async XLA Ops:
  0.6 33.1 %copy-start = (bf16[3,4,64,1024]{3,2,1,0:T(8,128)(2,1)S(1)}, bf16[3,4,64,1024]{3,2,1,0:T(8,128)(2,1)}, u32[]{:S(2)}) copy-start(bf16[3,4,64,1024]{3,2,1,0:T(8,128)(2,1)} %param.8) | copy-start | bytes 4718596
  0.6 1.1 copy-start.4
  1.7 0.9 copy-start.6
  33.8 4.3 %copy-start.9 = (s32[1,4]{1,0:T(1,128)S(1)}, s32[1,4]{1,0:T(1,128)}, u32[]{:S(2)}) copy-start(s32[1,4]{1,0:T(1,128)} %param.11) | copy-start | bytes 52
  33.8 4.4 %copy-start.7 = (bf16[64,1024]{1,0:T(8,128)(2,1)S(1)}, bf16[64,1024]{1,0:T(8,128)(2,1)}, u32[]{:S(2)}) copy-start(bf16[64,1024]{1,0:T(8,128)(2,1)} %param.7) | copy-start | bytes 393220
  38.1 1.4 copy-start.8
  41.2 3.1 %copy-start.10 = (s32[1,4]{1,0:T(1,128)S(1)}, s32[1,4]{1,0:T(1,128)}, u32[]{:S(2)}) copy-start(s32[1,4]{1,0:T(1,128)} %param.12) | copy-start | bytes 52
  93.5 1.3 copy-start.1
  94.9 2.6 %copy-start.2 = (bf16[2048,512]{1,0:T(8,128)(2,1)S(1)}, bf16[2048,512]{1,0:T(8,128)(2,1)}, u32[]{:S(2)}) copy-start(bf16[2048,512]{1,0:T(8,128)(2,1)} %copy-done.1) | copy-start | bytes 6291460
  133.3 0.7 copy-start.5
  173.6 2.5 %copy-start.3 = (bf16[2048,512]{1,0:T(8,128)(2,1)S(1)}, bf16[2048,512]{1,0:T(8,128)(2,1)}, u32[]{:S(2)}) copy-start(bf16[2048,512]{1,0:T(8,128)(2,1)} %copy-done.1) | copy-start | bytes 6291460

commit v4 on v3

--- a/solution.py
+++ b/solution.py
@@ -212,56 +212,88 @@
     )
 
 
-def relay(parts, count, place, far_sem, near_sem, side_sem, recv_sem):
+def relay(parts, count, place, far_sem, near_sem, side_sem, recv_sem, pair=True, between=None):
     row, col, core, sibling, far, near, _ = place
+    outer, inner = len(far) + 1, len(near) + 1
+    home, lane = col // inner, col % inner
     started = []
 
-    def send(part, block, sem, peer):
-        ref = parts(core, block)[part]
-        copy = remote(ref, ref, sem, recv_sem.at[part, core, block], peer)
-        copy.start()
-        started.append(copy)
-
-    def arrived(part, which, block):
-        ref = parts(which, block)[part]
-        remote(ref, ref, side_sem.at[part, 0], recv_sem.at[part, which, block], sibling).wait_recv()
-
-    def pass_on(part, block, step):
+    def send(part, block, sem, peer, valid=None):
+        def build():
+            ref = parts(core, block)[part]
+            return remote(ref, ref, sem, recv_sem.at[part, core, block], peer)
+
+        started.append((build, valid))
+        if valid is None:
+            build().start()
+        else:
+            pl.when(valid)(lambda: build().start())
+
+    def arrived(part, which, block, valid=None):
+        def wait():
+            ref = parts(which, block)[part]
+            sem = recv_sem.at[part, which, block]
+            remote(ref, ref, side_sem.at[part, 0], sem, sibling).wait_recv()
+
+        if valid is None:
+            wait()
+        else:
+            pl.when(valid)(wait)
+
+    def both(one, other):
+        return one if other is None else jnp.logical_and(one, other)
+
+    def onward(part, block, step, sign, valid=None):
+        target = home + sign
+        reached = jnp.logical_and(target >= 0, target < outer)
+        peer = (row, jnp.clip(target, 0, outer - 1) * inner + lane)
+        send(part, block, far_sem.at[part, step], peer, both(reached, valid))
+
+    def pass_on(part, block, step, valid=None):
         for e, peer in enumerate(near):
-            send(part, block, near_sem.at[part, step, e], peer)
-        send(part, block, side_sem.at[part, step], sibling)
+            send(part, block, near_sem.at[part, step, e], peer, valid)
+        if pair:
+            send(part, block, side_sem.at[part, step], sibling, valid)
 
     for part in range(count):
-        for d, peer in enumerate(far):
-            send(part, col, far_sem.at[part, d], peer)
-    for part in range(count):
+        onward(part, col, 0, -1)
+        onward(part, col, 1, 1)
         pass_on(part, col, 0)
-    outer, inner = len(far) + 1, len(near) + 1
+    if between is not None:
+        between()
     for d in range(1, outer):
-        block = far[d - 1][1]
-        for part in range(count):
-            arrived(part, core, block)
-            pass_on(part, block, d)
-    home, lane = col // inner, col % inner
+        for turn, sign in enumerate((-1, 1)):
+            source = home + sign * d
+            valid = jnp.logical_and(source >= 0, source < outer)
+            block = jnp.clip(source, 0, outer - 1) * inner + lane
+            for part in range(count):
+                arrived(part, core, block, valid)
+                onward(part, block, 2 * d + turn, -sign, valid)
+                pass_on(part, block, 2 * d + turn, valid)
     for d in range(outer):
         for e in range(1, inner):
             block = ((home + d) % outer) * inner + (lane + e) % inner
             for part in range(count):
                 arrived(part, core, block)
-                send(part, block, side_sem.at[part, e * outer + d], sibling)
-    for block in range(outer * inner):
-        for part in range(count):
-            arrived(part, 1 - core, block)
-    for copy in started:
-        copy.wait_send()
+                if pair:
+                    send(part, block, side_sem.at[part, 2 * outer + e * outer + d], sibling)
+    if pair:
+        for block in range(outer * inner):
+            for part in range(count):
+                arrived(part, 1 - core, block)
+    for build, valid in started:
+        if valid is None:
+            build().wait_send()
+        else:
+            pl.when(valid)(lambda build=build: build().wait_send())
 
 
 def relay_sems(count, col_count):
     outer, inner = split_axis(col_count)
     return [
-        pltpu.SemaphoreType.DMA((count, outer)),
-        pltpu.SemaphoreType.DMA((count, outer, inner)),
-        pltpu.SemaphoreType.DMA((count, col_count)),
+        pltpu.SemaphoreType.DMA((count, 2 * outer)),
+        pltpu.SemaphoreType.DMA((count, 2 * outer, inner)),
+        pltpu.SemaphoreType.DMA((count, 2 * outer + col_count)),
         pltpu.SemaphoreType.DMA((count, 2, col_count)),
     ]
 
@@ -322,13 +354,12 @@
     own_sem,
     row_send,
     row_recv,
-    far_send,
-    near_send,
-    panel_recv,
     trail_send,
     trail_recv,
+    *sems,
 ):
-    row, col, core, sibling, far, near, _ = here_and_peers(row_count, col_count)
+    place = here_and_peers(row_count, col_count)
+    row, col, core, sibling, far, near, _ = place
     panel_total = panel_ref.shape[1]
     trail_width = trail_ref.shape[1]
     slots = rows_ref.shape[0] // row_count
@@ -371,46 +402,37 @@
     for group in groups:
         arrived(held_ref.at[slot_range(group), sides[0]], row_recv.at[0, group])
     mine = held_ref.at[:, sides[0]]
-    for d, peer in enumerate(far):
-        send(mine, panel_ref.at[wide_range(col)], far_send.at[d], panel_recv.at[col], peer)
-    for e, peer in enumerate(near):
-        send(mine, panel_ref.at[wide_range(col)], near_send.at[0, e], panel_recv.at[col], peer)
     keep = pltpu.make_async_copy(mine, panel_ref.at[wide_range(col)], own_sem.at[1])
     keep.start()
-    for group in groups:
-        arrived(held_ref.at[slot_range(group), sides[1]], row_recv.at[1, group])
+    keep.wait()
 
     def trail_lanes(block):
         first = panel_total + block * trail_width
         return pl.ds(pl.multiple_of(first, trail_width), trail_width)
 
-    for d, other in enumerate(others):
-        send(
-            held_ref.at[:, trail_lanes(other)],
-            trail_ref.at[wide_range(col)],
-            trail_send.at[d],
-            trail_recv.at[col],
-            (row, other),
-        )
     keep_trail = pltpu.make_async_copy(
         held_ref.at[:, trail_lanes(col)], trail_ref.at[wide_range(col)], own_sem.at[2]
     )
-    keep_trail.start()
-    outer, inner = len(far) + 1, len(near) + 1
-    for d in range(1, outer):
-        block = far[d - 1][1]
-        ref = panel_ref.at[wide_range(block)]
-        arrived(ref, panel_recv.at[block])
-        for e, peer in enumerate(near):
-            send(ref, ref, near_send.at[d, e], panel_recv.at[block], peer)
-    home, lane = col // inner, col % inner
-    for d in range(outer):
-        for e in range(1, inner):
-            block = ((home + d) % outer) * inner + (lane + e) % inner
-            arrived(panel_ref.at[wide_range(block)], panel_recv.at[block])
+
+    def send_trail():
+        for group in groups:
+            arrived(held_ref.at[slot_range(group), sides[1]], row_recv.at[1, group])
+        for d, other in enumerate(others):
+            send(
+                held_ref.at[:, trail_lanes(other)],
+                trail_ref.at[wide_range(col)],
+                trail_send.at[d],
+                trail_recv.at[col],
+                (row, other),
+            )
+        keep_trail.start()
+
+    def parts(which, block):
+        return [panel_ref.at[wide_range(block)]]
+
+    relay(parts, 1, place, *sems, pair=False, between=send_trail)
     for other in others:
         arrived(trail_ref.at[wide_range(other)], trail_recv.at[other])
-    keep.wait()
     keep_trail.wait()
     for copy in started:
         copy.wait_send()
@@ -419,7 +441,6 @@
 def exchange_rows(kernel_rows, panel_total, row_count, col_count):
     total, env_count = kernel_rows.shape
     trail_width = (env_count - panel_total) // col_count
-    outer, inner = split_axis(col_count)
     return pl.pallas_call(
         lambda *refs: exchange_kernel(row_count, col_count, *refs),
         out_shape=(
@@ -433,11 +454,9 @@
             pltpu.SemaphoreType.DMA((3,)),
             pltpu.SemaphoreType.DMA((2, row_count)),
             pltpu.SemaphoreType.DMA((2, row_count)),
-            pltpu.SemaphoreType.DMA((outer,)),
-            pltpu.SemaphoreType.DMA((outer, inner)),
             pltpu.SemaphoreType.DMA((col_count,)),
             pltpu.SemaphoreType.DMA((col_count,)),
-            pltpu.SemaphoreType.DMA((col_count,)),
+            *relay_sems(1, col_count),
         ],
         compiler_params=pltpu.CompilerParams(
             collective_id=3, has_side_effects=True, vmem_limit_bytes=40 * 1024 * 1024

time: 178 us -> 161 us (0.904)
  Pallas kernels: 153 us -> 137 us
    pallas_call x1, Pallas kernels: 35.3 us -> 23.1 us  [sum_products(): pl.pallas_call(lambda *refs: sum_kernel(row_count, col_count, *refs), out...]
    pallas_call x1, Pallas kernels: 31.1 us -> 27.5 us  [gather_environments(): pl.pallas_call(lambda *refs: gather_kernel(row_count, col_count, *refs),...]
where the time goes in v4:
time: 161 us
  Pallas kernels  137 us (85%)
  matrix products  13.4 us (8%)
  local copies, waits for them, and re-layouts  6.67 us (4%)
  other arithmetic  3.69 us (2%)
    pallas_call x1, Pallas kernels, exchange_rows(): pl.pallas_call(lambda *refs: exchange_kernel(row_count, col_count, *refs)...  47.4 us
    pallas_call x1, Pallas kernels, factor_panel(): pl.pallas_call(lambda *refs: factor_kernel(total_rows, *refs), out_shape=...  38.6 us
    pallas_call x1, Pallas kernels, gather_environments(): pl.pallas_call(lambda *refs: gather_kernel(row_count, col_count, *refs),...  27.5 us
    pallas_call x1, Pallas kernels, sum_products(): pl.pallas_call(lambda *refs: sum_kernel(row_count, col_count, *refs), out...  23.1 us
    dot_general x2, matrix products, contract_rows(): lax.dot_general(left_side, right_side, (((1,), (1,)), ((), ())), preferre...  5.39 us
    unnamed x23, local copies, waits for them, and re-layouts  5.34 us

profile of v4, /device:TPU:0, one launch (start us, length us, event | category | flops | bytes accessed | tf_op | source)
XLA Modules:
  0.0 161.2 jit_solution(15208325965368302467)
XLA Ops:
  0.6 0.0 copy-start
  0.7 1.1 copy-done.4
  1.7 0.9 copy-done.6
  2.6 27.5 %gather_environments.1 = bf16[1536,1024]{1,0:T(8,128)(2,1)S(1)} custom-call(bf16[64,1024]{1,0:T(8,128)(2,1)S(1)} %copy-done.6, bf16[128,1024]{1,0:T(8,128)(2,1)S(1)} %copy-done.4), custom_call_target="tpu_custom_call" | custom-call | tf_op jit(solution)/shard_map/gather_environments/pallas_call | solution.py:334
  30.1 0.0 copy-start.9
  30.1 0.0 copy-start.7
  30.2 4.3 %fusion.21 = f32[1536,768]{0,1:T(8,128)} fusion(bf16[1536,1024]{1,0:T(8,128)(2,1)S(1)} %gather_environments.1, bf16[768,1024]{1,0:T(8,128)(2,1)S(1)} %bitcast.35), kind=kOutput, calls=%fused_computation.44 | convolution fusion | flops 2415919104 | bytes 9437184 | tf_op jit(solution)/shard_map/dot_general | solution.py:580
  34.4 0.1 fusion.14
  34.5 1.1 multiply_reduce_fusion.1
  35.6 0.1 fusion.13
  35.7 0.1 mul.82
  35.8 0.3 fusion.12
  36.1 0.1 reshape.221
  36.2 1.4 fusion.5
  37.6 0.0 copy-start.10
  37.6 3.0 %multiply_reduce_fusion = bf16[3,64,1536]{2,1,0:T(8,128)(2,1)S(1)} fusion(f32[3,4,64,1536]{3,2,1,0:T(8,128)} %bitcast.37, f32[4,64,1536]{2,1,0:T(8,128)S(1)} %fusion.5), kind=kLoop, calls=%fused_computation | loop fusion | flops 2064384 | bytes 6881280 | tf_op jit(solution)/shard_map/reduce_sum | solution.py:44
  40.6 0.1 divide_convert_fusion
  40.7 0.1 select_reduce_fusion
  40.9 0.1 select_select_fusion
  40.9 0.1 select_n.75
  41.0 0.4 convolution_convert_fusion.refs_0_
  41.4 47.4 %exchange_rows.1 = (bf16[2048,512]{1,0:T(8,128)(2,1)S(1)}, bf16[2048,128]{1,0:T(8,128)(2,1)S(1)}) custom-call(bf16[256,1536]{1,0:T(8,128)(2,1)S(1)} %convolution_convert_fusion.refs_0_), custom_call_target="tpu_custom_call" | custom-call | tf_op jit(solution)/shard_map/exchange_rows/pallas_call | solution.py:444
  88.9 1.3 copy-done.1
  90.2 2.6 %fusion.3.refs_0_ = f32[64,512]{1,0:T(8,128)S(1)} fusion(bf16[2048,512]{1,0:T(8,128)(2,1)} %copy-done.1, s32[]{:T(128)S(6)} %select_n.79), kind=kOutput, calls=%fused_computation.7 | convolution fusion | flops 134217728 | bytes 2752516 | tf_op jit(solution)/shard_map/dot_general | solution.py:586
  92.8 0.5 fusion.22.refs_1_
  93.3 23.1 %sum_products.1 = (f32[512,512]{1,0:T(8,128)S(1)}, f32[128,512]{1,0:T(8,128)S(1)}) custom-call(f32[64,512]{1,0:T(8,128)S(1)} %fusion.3.refs_0_, f32[128,512]{1,0:T(8,128)S(1)} %fusion.22.refs_1_), custom_call_target="tpu_custom_call" | custom-call | tf_op jit(solution)/shard_map/sum_products/pallas_call | solution.py:553
  116.4 0.7 copy-done.5
  117.1 1.1 copy.20
  118.2 38.6 %factor_panel.1 = (f32[512,512]{1,0:T(8,128)}, f32[128,512]{1,0:T(8,128)}, bf16[512,128]{1,0:T(8,128)(2,1)S(1)}, bf16[512,128]{1,0:T(8,128)(2,1)S(1)}) custom-call(f32[512,512]{1,0:T(8,128)S(1)} %get-tuple-element.13.refs_0_, f32[512,128]{1,0:T(8,128)S(1)} %bitcast.36), custom_call_target="tpu_custom_call" | custom-call | tf_op jit(solution)/shard_map/factor_panel/pallas_call | solution.py:156
  156.7 2.4 %convolution_subtract_fusion.1 = f32[128,2048]{0,1:T(8,128)S(1)} fusion(bf16[2048,512]{1,0:T(8,128)(2,1)} %copy-done.1, bf16[512,128]{1,0:T(8,128)(2,1)S(1)} %get-tuple-element.17, bf16[2048,128]{1,0:T(8,128)(2,1)S(1)} %get-tuple-element.12), kind=kOutput, calls=%fused_computation.3 | convolution fusion | flops 268959744 | bytes 3801088 | tf_op jit(solution)/shard_map/dot_general | solution.py:592
  159.2 0.7 convolution_subtract_fusion
  159.9 1.3 copy.23
  (21 shorter events, 0.1 us)
Async XLA Ops:
  0.6 29.5 %copy-start = (bf16[3,4,64,1024]{3,2,1,0:T(8,128)(2,1)S(1)}, bf16[3,4,64,1024]{3,2,1,0:T(8,128)(2,1)}, u32[]{:S(2)}) copy-start(bf16[3,4,64,1024]{3,2,1,0:T(8,128)(2,1)} %param.8) | copy-start | bytes 4718596
  0.6 1.1 copy-start.4
  1.7 0.9 copy-start.6
  30.1 4.3 %copy-start.9 = (s32[1,4]{1,0:T(1,128)S(1)}, s32[1,4]{1,0:T(1,128)}, u32[]{:S(2)}) copy-start(s32[1,4]{1,0:T(1,128)} %param.11) | copy-start | bytes 52
  30.1 4.4 %copy-start.7 = (bf16[64,1024]{1,0:T(8,128)(2,1)S(1)}, bf16[64,1024]{1,0:T(8,128)(2,1)}, u32[]{:S(2)}) copy-start(bf16[64,1024]{1,0:T(8,128)(2,1)} %param.7) | copy-start | bytes 393220
  34.4 1.4 copy-start.8
  37.6 3.1 %copy-start.10 = (s32[1,4]{1,0:T(1,128)S(1)}, s32[1,4]{1,0:T(1,128)}, u32[]{:S(2)}) copy-start(s32[1,4]{1,0:T(1,128)} %param.12) | copy-start | bytes 52
  88.9 1.3 copy-start.1
  90.2 2.6 %copy-start.2 = (bf16[2048,512]{1,0:T(8,128)(2,1)S(1)}, bf16[2048,512]{1,0:T(8,128)(2,1)}, u32[]{:S(2)}) copy-start(bf16[2048,512]{1,0:T(8,128)(2,1)} %copy-done.1) | copy-start | bytes 6291460
  116.4 0.7 copy-start.5
  156.7 2.5 %copy-start.3 = (bf16[2048,512]{1,0:T(8,128)(2,1)S(1)}, bf16[2048,512]{1,0:T(8,128)(2,1)}, u32[]{:S(2)}) copy-start(bf16[2048,512]{1,0:T(8,128)(2,1)} %copy-done.1) | copy-start | bytes 6291460

commit v5 on v4

--- a/solution.py
+++ b/solution.py
@@ -59,7 +59,7 @@
     ).astype(jnp.bfloat16)
 
 
-GROUP = 8
+GROUP = 16
 BLOCK = 128
 
 
@@ -116,7 +116,7 @@
     col_ids = lax.broadcasted_iota(jnp.int32, (BLOCK, BLOCK), 1)
     unit = (row_ids == col_ids).astype(jnp.float32)
     field_ref[:, :size] = gram_ref[...] / total_rows
-    field_ref[:, size:] = cross_ref[...] / total_rows
+    field_ref[:, size:] = cross_ref[...].T / total_rows
     factor_ref[...] = jnp.zeros_like(factor_ref)
     for b in range(blocks):
         here = slice(b * BLOCK, (b + 1) * BLOCK)
@@ -152,7 +152,7 @@
 
 
 def factor_panel(gram_sum, cross_sum, total_rows):
-    size, width = cross_sum.shape
+    width, size = cross_sum.shape
     return pl.pallas_call(
         lambda *refs: factor_kernel(total_rows, *refs),
         out_shape=(
@@ -616,7 +616,6 @@
     gram_sum, cross_sum = sum_products(
         contract_cols(panel_own, segment), contract_cols(trail_own, segment), row_count, col_count
     )
-    cross_sum = cross_sum.T
     panel_factor, cross_factor, weight_high, weight_low = factor_panel(
         gram_sum, cross_sum, total_rows
     )

time: 161 us -> 146 us (0.907)
  Pallas kernels: 137 us -> 124 us
  local copies, waits for them, and re-layouts: 6.67 us -> 4.91 us
  matrix products: 13.4 us -> 11.7 us
    pallas_call x1, Pallas kernels: 38.6 us -> 26.3 us  [factor_panel(): pl.pallas_call(lambda *refs: factor_kernel(total_rows, *refs), out_shape=...]
    dot_general x2, matrix products: 3.14 us -> 1.41 us  [project(): lax.dot_general(weights, segment, (((0,), (1,)), ((), ())), preferred_ele...]
    unnamed x23 -> x19, local copies, waits for them, and re-layouts: 5.34 us -> 4.65 us
where the time goes in v5:
time: 146 us; the launch traced here: 145 us
  Pallas kernels  124 us (85%)
  matrix products  11.7 us (8%)
  local copies, waits for them, and re-layouts  4.91 us (3%)
  other arithmetic  3.69 us (3%)
    pallas_call x1, Pallas kernels, exchange_rows(): pl.pallas_call(lambda *refs: exchange_kernel(row_count, col_count, *refs)...  47.4 us
    pallas_call x1, Pallas kernels, gather_environments(): pl.pallas_call(lambda *refs: gather_kernel(row_count, col_count, *refs),...  27.5 us
    pallas_call x1, Pallas kernels, factor_panel(): pl.pallas_call(lambda *refs: factor_kernel(total_rows, *refs), out_shape=...  26.3 us
    pallas_call x1, Pallas kernels, sum_products(): pl.pallas_call(lambda *refs: sum_kernel(row_count, col_count, *refs), out...  23.1 us
    dot_general x2, matrix products, contract_rows(): lax.dot_general(left_side, right_side, (((1,), (1,)), ((), ())), preferre...  5.38 us
    unnamed x19, local copies, waits for them, and re-layouts  4.65 us
    dot_general x2, matrix products, contract_cols(): lax.dot_general(left_side, right_side, (((0,), (0,)), ((), ())), preferre...  3.06 us
    reduce_sum x1, other arithmetic, slot_rows(): forces = jnp.sum(picked * slope_dots, axis=1).reshape(3 * atoms, env_count)  2.97 us

profile of v5, /device:TPU:0, one launch (start us, length us, event | category | flops | bytes accessed | tf_op | source)
XLA Modules:
  0.0 145.4 jit_solution(815622507271039302)
XLA Ops:
  0.6 0.0 copy-start
  0.7 1.1 copy-done.3
  1.7 0.9 copy-done.4
  2.6 27.5 %gather_environments.1 = bf16[1536,1024]{1,0:T(8,128)(2,1)S(1)} custom-call(bf16[64,1024]{1,0:T(8,128)(2,1)S(1)} %copy-done.4, bf16[128,1024]{1,0:T(8,128)(2,1)S(1)} %copy-done.3), custom_call_target="tpu_custom_call" | custom-call | tf_op jit(solution)/shard_map/gather_environments/pallas_call | solution.py:334
  30.1 0.0 copy-done
  30.1 0.0 copy-start.7
  30.1 0.0 copy-start.5
  30.2 4.3 %fusion.21 = f32[1536,768]{0,1:T(8,128)} fusion(bf16[1536,1024]{1,0:T(8,128)(2,1)S(1)} %gather_environments.1, bf16[768,1024]{1,0:T(8,128)(2,1)S(1)} %bitcast.34), kind=kOutput, calls=%fused_computation.44 | convolution fusion | flops 2415919104 | bytes 9437184 | tf_op jit(solution)/shard_map/dot_general | solution.py:580
  34.4 0.1 fusion.14
  34.5 0.0 copy-done.5
  34.5 1.1 multiply_reduce_fusion.1
  35.6 0.1 fusion.13
  35.7 0.1 mul.82
  35.8 0.3 fusion.12
  36.1 0.1 reshape.221
  36.2 1.4 fusion.5
  37.6 0.0 copy-start.8
  37.6 3.0 %multiply_reduce_fusion = bf16[3,64,1536]{2,1,0:T(8,128)(2,1)S(1)} fusion(f32[3,4,64,1536]{3,2,1,0:T(8,128)} %bitcast.35, f32[4,64,1536]{2,1,0:T(8,128)S(1)} %fusion.5), kind=kLoop, calls=%fused_computation | loop fusion | flops 2064384 | bytes 6881280 | tf_op jit(solution)/shard_map/reduce_sum | solution.py:44
  40.6 0.1 divide_convert_fusion
  40.7 0.1 select_reduce_fusion
  40.8 0.1 select_select_fusion
  40.9 0.1 select_n.75
  41.0 0.4 convolution_convert_fusion.refs_0_
  41.4 47.4 %exchange_rows.1 = (bf16[2048,512]{1,0:T(8,128)(2,1)S(1)}, bf16[2048,128]{1,0:T(8,128)(2,1)S(1)}) custom-call(bf16[256,1536]{1,0:T(8,128)(2,1)S(1)} %convolution_convert_fusion.refs_0_), custom_call_target="tpu_custom_call" | custom-call | tf_op jit(solution)/shard_map/exchange_rows/pallas_call | solution.py:444
  88.9 1.3 copy-done.1
  90.2 2.6 %fusion.3.refs_0_ = f32[64,512]{1,0:T(8,128)S(1)} fusion(bf16[2048,512]{1,0:T(8,128)(2,1)} %copy-done.1, s32[]{:T(128)S(6)} %select_n.79), kind=kOutput, calls=%fused_computation.7 | convolution fusion | flops 134217728 | bytes 2752516 | tf_op jit(solution)/shard_map/dot_general | solution.py:586
  92.8 0.5 fusion.22.refs_1_
  93.3 23.1 %sum_products.1 = (f32[512,512]{1,0:T(8,128)S(1)}, f32[128,512]{1,0:T(8,128)S(1)}) custom-call(f32[64,512]{1,0:T(8,128)S(1)} %fusion.3.refs_0_, f32[128,512]{1,0:T(8,128)S(1)} %fusion.22.refs_1_), custom_call_target="tpu_custom_call" | custom-call | tf_op jit(solution)/shard_map/sum_products/pallas_call | solution.py:553
  116.4 26.3 %factor_panel.1 = (f32[512,512]{1,0:T(8,128)}, f32[128,512]{1,0:T(8,128)}, bf16[512,128]{1,0:T(8,128)(2,1)S(1)}, bf16[512,128]{1,0:T(8,128)(2,1)S(1)}) custom-call(f32[512,512]{1,0:T(8,128)S(1)} %get-tuple-element.13.refs_0_, f32[128,512]{1,0:T(8,128)S(1)} %get-tuple-element.14.refs_1_), custom_call_target="tpu_custom_call" | custom-call | tf_op jit(solution)/shard_map/factor_panel/pallas_call | solution.py:156
  142.7 0.7 convolution_subtract_fusion.1
  143.4 0.7 convolution_subtract_fusion
  144.1 1.3 copy.20
  (16 shorter events, 0.1 us)
Async XLA Ops:
  0.6 29.5 %copy-start = (bf16[3,4,64,1024]{3,2,1,0:T(8,128)(2,1)S(1)}, bf16[3,4,64,1024]{3,2,1,0:T(8,128)(2,1)}, u32[]{:S(2)}) copy-start(bf16[3,4,64,1024]{3,2,1,0:T(8,128)(2,1)} %param.8) | copy-start | bytes 4718596
  0.6 1.1 copy-start.3
  1.7 0.9 copy-start.4
  30.1 4.3 %copy-start.7 = (s32[1,4]{1,0:T(1,128)S(1)}, s32[1,4]{1,0:T(1,128)}, u32[]{:S(2)}) copy-start(s32[1,4]{1,0:T(1,128)} %param.11) | copy-start | bytes 52
  30.1 4.4 %copy-start.5 = (bf16[64,1024]{1,0:T(8,128)(2,1)S(1)}, bf16[64,1024]{1,0:T(8,128)(2,1)}, u32[]{:S(2)}) copy-start(bf16[64,1024]{1,0:T(8,128)(2,1)} %param.7) | copy-start | bytes 393220
  34.4 1.4 copy-start.6
  37.6 3.1 %copy-start.8 = (s32[1,4]{1,0:T(1,128)S(1)}, s32[1,4]{1,0:T(1,128)}, u32[]{:S(2)}) copy-start(s32[1,4]{1,0:T(1,128)} %param.12) | copy-start | bytes 52
  88.9 1.3 copy-start.1
  90.2 2.6 %copy-start.2 = (bf16[2048,512]{1,0:T(8,128)(2,1)S(1)}, bf16[2048,512]{1,0:T(8,128)(2,1)}, u32[]{:S(2)}) copy-start(bf16[2048,512]{1,0:T(8,128)(2,1)} %copy-done.1) | copy-start | bytes 6291460

commit v6 on v5

--- a/solution.py
+++ b/solution.py
@@ -59,7 +59,7 @@
     ).astype(jnp.bfloat16)
 
 
-GROUP = 16
+GROUP = 32
 BLOCK = 128
 
 

time: 146 us -> 143 us (0.979)
  Pallas kernels: 124 us -> 122 us
    pallas_call x1, Pallas kernels: 26.3 us -> 23.6 us  [factor_panel(): pl.pallas_call(lambda *refs: factor_kernel(total_rows, *refs), out_shape=...]
where the time goes in v6:
time: 143 us
  Pallas kernels  122 us (85%)
  matrix products  11.7 us (8%)
  local copies, waits for them, and re-layouts  4.91 us (3%)
  other arithmetic  3.69 us (3%)
    pallas_call x1, Pallas kernels, exchange_rows(): pl.pallas_call(lambda *refs: exchange_kernel(row_count, col_count, *refs)...  47.4 us
    pallas_call x1, Pallas kernels, gather_environments(): pl.pallas_call(lambda *refs: gather_kernel(row_count, col_count, *refs),...  27.5 us
    pallas_call x1, Pallas kernels, factor_panel(): pl.pallas_call(lambda *refs: factor_kernel(total_rows, *refs), out_shape=...  23.6 us
    pallas_call x1, Pallas kernels, sum_products(): pl.pallas_call(lambda *refs: sum_kernel(row_count, col_count, *refs), out...  23.1 us
    dot_general x2, matrix products, contract_rows(): lax.dot_general(left_side, right_side, (((1,), (1,)), ((), ())), preferre...  5.38 us
    unnamed x19, local copies, waits for them, and re-layouts  4.65 us
    dot_general x2, matrix products, contract_cols(): lax.dot_general(left_side, right_side, (((0,), (0,)), ((), ())), preferre...  3.06 us
    reduce_sum x1, other arithmetic, slot_rows(): forces = jnp.sum(picked * slope_dots, axis=1).reshape(3 * atoms, env_count)  2.97 us

profile of v6, /device:TPU:0, one launch (start us, length us, event | category | flops | bytes accessed | tf_op | source)
XLA Modules:
  0.0 142.7 jit_solution(16335694072086919059)
XLA Ops:
  0.6 0.0 copy-start
  0.6 0.0 copy-start.3
  0.7 1.1 copy-done.3
  1.7 0.9 copy-done.4
  2.6 27.5 %gather_environments.1 = bf16[1536,1024]{1,0:T(8,128)(2,1)S(1)} custom-call(bf16[64,1024]{1,0:T(8,128)(2,1)S(1)} %copy-done.4, bf16[128,1024]{1,0:T(8,128)(2,1)S(1)} %copy-done.3), custom_call_target="tpu_custom_call" | custom-call | tf_op jit(solution)/shard_map/gather_environments/pallas_call | solution.py:334
  30.1 0.0 copy-start.7
  30.1 0.0 copy-start.5
  30.2 4.3 %fusion.21 = f32[1536,768]{0,1:T(8,128)} fusion(bf16[1536,1024]{1,0:T(8,128)(2,1)S(1)} %gather_environments.1, bf16[768,1024]{1,0:T(8,128)(2,1)S(1)} %bitcast.34), kind=kOutput, calls=%fused_computation.44 | convolution fusion | flops 2415919104 | bytes 9437184 | tf_op jit(solution)/shard_map/dot_general | solution.py:580
  34.4 0.0 copy-done.7
  34.4 0.1 fusion.14
  34.5 1.1 multiply_reduce_fusion.1
  35.6 0.1 fusion.13
  35.7 0.1 mul.82
  35.8 0.3 fusion.12
  36.1 0.1 reshape.221
  36.2 1.4 fusion.5
  37.6 0.0 copy-start.8
  37.6 3.0 %multiply_reduce_fusion = bf16[3,64,1536]{2,1,0:T(8,128)(2,1)S(1)} fusion(f32[3,4,64,1536]{3,2,1,0:T(8,128)} %bitcast.35, f32[4,64,1536]{2,1,0:T(8,128)S(1)} %fusion.5), kind=kLoop, calls=%fused_computation | loop fusion | flops 2064384 | bytes 6881280 | tf_op jit(solution)/shard_map/reduce_sum | solution.py:44
  40.6 0.1 divide_convert_fusion
  40.7 0.1 select_reduce_fusion
  40.8 0.1 select_select_fusion
  40.9 0.1 select_n.75
  41.0 0.4 convolution_convert_fusion.refs_0_
  41.4 47.4 %exchange_rows.1 = (bf16[2048,512]{1,0:T(8,128)(2,1)S(1)}, bf16[2048,128]{1,0:T(8,128)(2,1)S(1)}) custom-call(bf16[256,1536]{1,0:T(8,128)(2,1)S(1)} %convolution_convert_fusion.refs_0_), custom_call_target="tpu_custom_call" | custom-call | tf_op jit(solution)/shard_map/exchange_rows/pallas_call | solution.py:444
  88.9 1.3 copy-done.1
  90.2 2.6 %fusion.3.refs_0_ = f32[64,512]{1,0:T(8,128)S(1)} fusion(bf16[2048,512]{1,0:T(8,128)(2,1)} %copy-done.1, s32[]{:T(128)S(6)} %select_n.79), kind=kOutput, calls=%fused_computation.7 | convolution fusion | flops 134217728 | bytes 2752516 | tf_op jit(solution)/shard_map/dot_general | solution.py:586
  92.8 0.5 fusion.22.refs_1_
  93.3 23.1 %sum_products.1 = (f32[512,512]{1,0:T(8,128)S(1)}, f32[128,512]{1,0:T(8,128)S(1)}) custom-call(f32[64,512]{1,0:T(8,128)S(1)} %fusion.3.refs_0_, f32[128,512]{1,0:T(8,128)S(1)} %fusion.22.refs_1_), custom_call_target="tpu_custom_call" | custom-call | tf_op jit(solution)/shard_map/sum_products/pallas_call | solution.py:553
  116.4 23.6 %factor_panel.1 = (f32[512,512]{1,0:T(8,128)}, f32[128,512]{1,0:T(8,128)}, bf16[512,128]{1,0:T(8,128)(2,1)S(1)}, bf16[512,128]{1,0:T(8,128)(2,1)S(1)}) custom-call(f32[512,512]{1,0:T(8,128)S(1)} %get-tuple-element.13.refs_0_, f32[128,512]{1,0:T(8,128)S(1)} %get-tuple-element.14.refs_1_), custom_call_target="tpu_custom_call" | custom-call | tf_op jit(solution)/shard_map/factor_panel/pallas_call | solution.py:156
  140.0 0.7 convolution_subtract_fusion.1
  140.7 0.7 convolution_subtract_fusion
  141.4 1.3 copy.20
  (16 shorter events, 0.1 us)
Async XLA Ops:
  0.6 29.5 %copy-start = (bf16[3,4,64,1024]{3,2,1,0:T(8,128)(2,1)S(1)}, bf16[3,4,64,1024]{3,2,1,0:T(8,128)(2,1)}, u32[]{:S(2)}) copy-start(bf16[3,4,64,1024]{3,2,1,0:T(8,128)(2,1)} %param.8) | copy-start | bytes 4718596
  0.6 1.1 copy-start.3
  1.7 0.9 copy-start.4
  30.1 4.3 %copy-start.7 = (s32[1,4]{1,0:T(1,128)S(1)}, s32[1,4]{1,0:T(1,128)}, u32[]{:S(2)}) copy-start(s32[1,4]{1,0:T(1,128)} %param.11) | copy-start | bytes 52
  30.1 4.4 %copy-start.5 = (bf16[64,1024]{1,0:T(8,128)(2,1)S(1)}, bf16[64,1024]{1,0:T(8,128)(2,1)}, u32[]{:S(2)}) copy-start(bf16[64,1024]{1,0:T(8,128)(2,1)} %param.7) | copy-start | bytes 393220
  34.4 1.4 copy-start.6
  37.6 3.1 %copy-start.8 = (s32[1,4]{1,0:T(1,128)S(1)}, s32[1,4]{1,0:T(1,128)}, u32[]{:S(2)}) copy-start(s32[1,4]{1,0:T(1,128)} %param.12) | copy-start | bytes 52
  88.9 1.3 copy-start.1
  90.2 2.6 %copy-start.2 = (bf16[2048,512]{1,0:T(8,128)(2,1)S(1)}, bf16[2048,512]{1,0:T(8,128)(2,1)}, u32[]{:S(2)}) copy-start(bf16[2048,512]{1,0:T(8,128)(2,1)} %copy-done.1) | copy-start | bytes 6291460
